TPU v7x, 32 devices: a whole 2x2x4 slice. The times are simulated.
32 devices in a mesh: seq: 4 (over x, core), tensor: 8 (over z, y).
Axes of the slice: x: 2, y: 2, z: 4, core: 2. Of those that a mesh axis runs over, the one named last changes fastest.
Arguments:
- tokens: bfloat16 [256, 2048], P(('seq', 'tensor')), may hold values from -6 to 6
- attn_gain: bfloat16 [2048], replicated, may hold values from 0.25 to 1.75
- w_qkv: bfloat16 [2048, 3, 2048], P(None, None, 'tensor'), may hold values from -0.125 to 0.125
- q_gain: bfloat16 [2048], P('tensor'), may hold values from 0.25 to 1.75
- k_gain: bfloat16 [2048], P('tensor'), may hold values from 0.25 to 1.75
- w_out: bfloat16 [2048, 2048], P('tensor'), may hold values from -0.125 to 0.125
- prefix_keys: bfloat16 [4, 2048, 2048], P('seq', None, 'tensor'), may hold values from -150 to 150
- prefix_values: bfloat16 [4, 2048, 2048], P('seq', None, 'tensor'), may hold values from -6 to 6
- segments: int32 [256], replicated, may hold values from 0 to 15, never falling along the last dimension, each value on 1 to 64 neighbouring positions
- request_group: int32 [16], replicated, may hold values from 0 to 1
- prefix_owner: int32 [2], replicated, may hold values from 0 to 3, as said below
- mlp_gain: bfloat16 [2048], replicated, may hold values from 0.25 to 1.75
- expert_ids: int32 [256, 8], P(('seq', 'tensor')), may hold values from 0 to 15, all different within a row; in each aligned block of 8 rows (0 to 7, 8 to 15, ...) at most 8 rows name the same one
- gate_weights: float32 [256, 8], P(('seq', 'tensor')), may hold values from 0.05 to 0.5
- w_gate: bfloat16 [32, 2048, 512], P(('tensor', 'seq')), may hold values from -0.125 to 0.125
- w_up: bfloat16 [32, 2048, 512], P(('tensor', 'seq')), may hold values from -0.125 to 0.125
- w_down: bfloat16 [32, 512, 2048], P(('tensor', 'seq')), may hold values from -0.1875 to 0.1875
Outputs:
- output: bfloat16 [256, 2048], P(('seq', 'tensor'))
- new_keys: bfloat16 [256, 2048], P('seq', 'tensor')
- new_values: bfloat16 [256, 2048], P('seq', 'tensor')
Inputs may be any that keep to these rules, and one draw needn't show every extreme that they name: `segments`: each request's tokens are consecutive; a request has at most 64 tokens, and some request has exactly 64. `prefix_owner`: distinct slots. `expert_ids`: a token's experts are distinct; among the 8 rows of one device no expert is named more than 8 times, and that count is reached.
All inputs are finite; a program needn't handle non-finite values.
Results may differ from a plain program's by a relative error of at most 0.017.
Values may be sent and summed in bfloat16 or wider, within the bound.
A program may use at most 64 MiB of HBM per device.

v0:
```python
import jax
import jax.numpy as jnp
from jax import lax
from jax.sharding import PartitionSpec as P

HD = 128
TOP = 8
EXP_DEV = 2


def from_partner(value, axis, stride):
    mask = 2**stride
    pairs = [(source, source ^ mask) for source in range(lax.axis_size(axis))]
    return lax.ppermute(value, axis, pairs)


def passed_along(value, axis, by):
    devices = lax.axis_size(axis)
    pairs = [(i, i + by) for i in range(devices) if 0 <= i + by < devices]
    return lax.ppermute(value, axis, pairs)


def rms_scale(values, gain):
    mean_square = jnp.mean(values * values, axis=-1, keepdims=True)
    return values * lax.rsqrt(mean_square + 1e-05) * gain.astype(jnp.float32)


def attend_block(carry, queries_heads, block, mask):
    largest, total, accum = carry
    heads_local = queries_heads.shape[1]
    count = block.shape[0]
    key_block = block[:, 0].reshape(count, heads_local, HD)
    value_block = block[:, 1].reshape(count, heads_local, HD)
    scores = jnp.einsum(
        "qhd,khd->hqk", queries_heads, key_block, preferred_element_type=jnp.float32
    ) * HD ** (-0.5)
    scores = jnp.where(mask[None], scores, -1e30)
    new_largest = jnp.maximum(largest, jnp.max(scores, axis=-1))
    weights = jnp.where(mask[None], jnp.exp(scores - new_largest[:, :, None]), 0.0)
    factor = jnp.exp(largest - new_largest)
    total = total * factor + jnp.sum(weights, axis=-1)
    update = jnp.einsum(
        "hqk,khd->hqd",
        weights.astype(jnp.bfloat16),
        value_block,
        preferred_element_type=jnp.float32,
    )
    accum = accum * factor[:, :, None] + update
    return (new_largest, total, accum)


def local(
    tokens,
    attn_gain,
    w_qkv,
    q_gain,
    k_gain,
    w_out,
    prefix_keys,
    prefix_values,
    segments,
    request_group,
    prefix_owner,
    mlp_gain,
    expert_ids,
    gate_weights,
    w_gate,
    w_up,
    w_down,
):
    tensor_size = lax.axis_size("tensor")
    seq_size = lax.axis_size("seq")
    seq_index = lax.axis_index("seq")
    tensor_index = lax.axis_index("tensor")
    tok_dev = tokens.shape[0]
    width = tokens.shape[1]
    tok_seq = tok_dev * tensor_size
    columns = w_qkv.shape[2]
    paired = columns < HD
    normed = rms_scale(tokens.astype(jnp.float32), attn_gain).astype(jnp.bfloat16)
    w_flat = w_qkv.reshape(width, 3 * columns)
    projected = jnp.dot(
        lax.all_gather(normed, "tensor", axis=0, tiled=True),
        w_flat,
        preferred_element_type=jnp.float32,
    )
    query_part = projected[:, :columns]
    key_part = projected[:, columns : 2 * columns]
    squares = lax.psum(
        (jnp.sum(query_part * query_part, axis=-1), jnp.sum(key_part * key_part, axis=-1)), "tensor"
    )
    query_rows = (
        query_part * lax.rsqrt(squares[0] / width + 1e-05)[:, None] * q_gain.astype(jnp.float32)
    ).astype(jnp.bfloat16)
    new_keys = (
        key_part * lax.rsqrt(squares[1] / width + 1e-05)[:, None] * k_gain.astype(jnp.float32)
    ).astype(jnp.bfloat16)
    new_values = projected[:, 2 * columns :].astype(jnp.bfloat16)
    stacked = jnp.stack(
        [
            jnp.concatenate([new_keys, prefix_keys[0]], axis=0),
            jnp.concatenate([new_values, prefix_values[0]], axis=0),
        ],
        axis=1,
    )
    half_rows = tok_seq // 2
    if paired:
        lower_bit = tensor_index % 2
        partner = from_partner(stacked, "tensor", 0)
        full = jnp.where(
            lower_bit == 0,
            jnp.concatenate([stacked, partner], axis=-1),
            jnp.concatenate([partner, stacked], axis=-1),
        )
        query_halves = query_rows.reshape(2, half_rows, columns)
        own_half = lax.dynamic_index_in_dim(query_halves, lower_bit, 0, keepdims=False)
        send_half = lax.dynamic_index_in_dim(query_halves, 1 - lower_bit, 0, keepdims=False)
        got_half = from_partner(send_half, "tensor", 0)
        query_full = jnp.where(
            lower_bit == 0,
            jnp.concatenate([own_half, got_half], axis=-1),
            jnp.concatenate([got_half, own_half], axis=-1),
        )
        query_count = half_rows
        query_offset = lower_bit * half_rows
        heads_local = 1
    else:
        full = stacked
        query_full = query_rows
        query_count = tok_seq
        query_offset = jnp.int32(0)
        heads_local = columns // HD
    suffix_full = full[:tok_seq]
    prefix_full = full[tok_seq:]
    queries_heads = query_full.reshape(query_count, heads_local, HD)
    groups_count = prefix_owner.shape[0]
    request_count = request_group.shape[0]
    token_group = jnp.sum(
        jnp.where(
            segments[:, None] == jnp.arange(request_count, dtype=jnp.int32)[None, :],
            request_group[None, :],
            0,
        ),
        axis=1,
    )
    base_row = seq_index * tok_seq
    query_start = base_row + query_offset
    query_seg = lax.dynamic_slice_in_dim(segments, query_start, query_count, 0)
    query_group = lax.dynamic_slice_in_dim(token_group, query_start, query_count, 0)
    query_pos = query_start + jnp.arange(query_count, dtype=jnp.int32)
    padded_seg = jnp.concatenate([jnp.full((tok_seq,), -1, jnp.int32), segments], axis=0)
    key_seg = lax.dynamic_slice_in_dim(padded_seg, base_row, 2 * tok_seq, 0)
    key_pos = base_row - tok_seq + jnp.arange(2 * tok_seq, dtype=jnp.int32)
    previous = passed_along(suffix_full, "seq", 1)
    suffix_keys = jnp.concatenate([previous, suffix_full], axis=0)
    suffix_mask = (key_seg[None, :] == query_seg[:, None]) & (
        key_pos[None, :] <= query_pos[:, None]
    )
    carry = (
        jnp.full((heads_local, query_count), -1e30, jnp.float32),
        jnp.zeros((heads_local, query_count), jnp.float32),
        jnp.zeros((heads_local, query_count, HD), jnp.float32),
    )
    carry = attend_block(carry, queries_heads, suffix_keys, suffix_mask)
    owner_of_query = jnp.sum(
        jnp.where(
            query_group[:, None] == jnp.arange(groups_count, dtype=jnp.int32)[None, :],
            prefix_owner[None, :],
            0,
        ),
        axis=1,
    )
    state = carry
    piece = lax.all_gather(prefix_full[None], "seq", axis=0, tiled=True)
    start = jnp.int32(0)
    for offset in range(piece.shape[0]):
        slot_mask = (owner_of_query == start + offset)[:, None]
        state = attend_block(state, queries_heads, piece[offset], slot_mask)
    carry = state
    attended = (carry[2] / carry[1][:, :, None]).astype(jnp.bfloat16)
    attended = jnp.transpose(attended, (1, 0, 2)).reshape(query_count, heads_local * HD)
    if paired:
        split_out = attended.reshape(query_count, 2, columns)
        own_out = lax.dynamic_index_in_dim(split_out, lower_bit, 1, keepdims=False)
        send_out = lax.dynamic_index_in_dim(split_out, 1 - lower_bit, 1, keepdims=False)
        got_out = from_partner(send_out, "tensor", 0)
        attended_local = jnp.where(
            lower_bit == 0,
            jnp.concatenate([own_out, got_out], axis=0),
            jnp.concatenate([got_out, own_out], axis=0),
        )
    else:
        attended_local = attended
    attn_sum = lax.psum_scatter(
        jnp.dot(attended_local, w_out, preferred_element_type=jnp.float32).astype(jnp.bfloat16),
        "tensor",
        scatter_dimension=0,
        tiled=True,
    ).astype(jnp.float32)
    mixed_rows = (tokens.astype(jnp.float32) + attn_sum).astype(jnp.bfloat16)
    expert_in = rms_scale(mixed_rows.astype(jnp.float32), mlp_gain).astype(jnp.bfloat16)
    exp_local = EXP_DEV
    experts_all = exp_local * tensor_size
    own_expert = seq_index // (seq_size // exp_local)
    capacity = max(2, 2 * tok_dev * TOP // experts_all)
    flat_ids = expert_ids.reshape(-1)
    onehot = (flat_ids[:, None] == jnp.arange(experts_all, dtype=jnp.int32)[None, :]).astype(
        jnp.int32
    )
    before = jnp.cumsum(onehot, axis=0) - onehot
    slot = flat_ids * capacity + jnp.sum(before * onehot, axis=1)
    slot_match = (
        slot.reshape(tok_dev, TOP)[:, :, None]
        == jnp.arange(experts_all * capacity, dtype=jnp.int32)[None, None, :]
    )
    dispatch_table = jnp.transpose(jnp.any(slot_match, axis=1)).astype(jnp.bfloat16)
    combine_table = jnp.sum(jnp.where(slot_match, gate_weights[:, :, None], 0.0), axis=1)
    buffer = jnp.dot(dispatch_table, expert_in, preferred_element_type=jnp.float32).astype(
        jnp.bfloat16
    )
    buffer = buffer.reshape(tensor_size, exp_local, capacity, width)
    received = lax.all_to_all(buffer, "tensor", split_axis=0, concat_axis=0, tiled=True)
    gate_local = w_gate[0]
    up_local = w_up[0]
    down_local = w_down[0]
    keep_expert = (jnp.arange(exp_local, dtype=jnp.int32) == own_expert)[None, None, :, None, None]
    chosen = lax.dynamic_index_in_dim(
        lax.all_gather(received[None], "seq", axis=0, tiled=True), own_expert, 2, keepdims=False
    )
    gated = jnp.einsum("srcd,df->srcf", chosen, gate_local, preferred_element_type=jnp.float32)
    upward = jnp.einsum("srcd,df->srcf", chosen, up_local, preferred_element_type=jnp.float32)
    activity = (jax.nn.silu(gated) * upward).astype(jnp.bfloat16)
    result = jnp.einsum("srcf,fd->srcd", activity, down_local, preferred_element_type=jnp.float32)
    partials = jnp.where(keep_expert, result[:, :, None], 0.0)
    summed = lax.psum_scatter(
        partials.astype(jnp.bfloat16), "seq", scatter_dimension=0, tiled=True
    ).astype(jnp.float32)
    returned = lax.all_to_all(
        summed[0].astype(jnp.bfloat16), "tensor", split_axis=0, concat_axis=0, tiled=True
    ).astype(jnp.float32)
    moe_sum = jnp.dot(
        combine_table,
        returned.reshape(experts_all * capacity, width),
        preferred_element_type=jnp.float32,
        precision=lax.Precision.HIGHEST,
    )
    output = (mixed_rows.astype(jnp.float32) + moe_sum).astype(jnp.bfloat16)
    return (output, new_keys, new_values)


def solution(mesh):
    return jax.shard_map(
        local,
        mesh=mesh,
        in_specs=(
            P(("seq", "tensor"), None),
            P(),
            P(None, None, "tensor"),
            P("tensor"),
            P("tensor"),
            P("tensor", None),
            P("seq", None, "tensor"),
            P("seq", None, "tensor"),
            P(),
            P(),
            P(),
            P(),
            P(("seq", "tensor"), None),
            P(("seq", "tensor"), None),
            P(("tensor", "seq"), None, None),
            P(("tensor", "seq"), None, None),
            P(("tensor", "seq"), None, None),
        ),
        out_specs=(P(("seq", "tensor"), None), P("seq", "tensor"), P("seq", "tensor")),
        check_vma=False,
    )
```

profile of v0, /device:TPU:0, one launch (start us, length us, event | category | flops | bytes accessed | tf_op | source)
XLA Modules:
  0.0 316.5 jit_solution(1087826893271445862)
XLA Ops:
  7.2 4.8 %copy.70 = bf16[2048,3,256]{0,2,1:T(8,128)(2,1)} copy(bf16[2048,3,256]{2,0,1:T(8,128)(2,1)} %param.19) | data formatting | bytes 6291456 | tf_op args[2]
  12.3 32.5 %all_gather.9 = bf16[64,2048]{1,0:T(8,128)(2,1)S(1)} all-gather(bf16[8,2048]{1,0:T(8,128)(2,1)S(1)} %fusion.70), channel_id=1, replica_groups=mesh['seq'=4,'tensor'=8] {'tensor'}, dimensions={0}, use_global_device_ids=true | all-gather | bytes 294912 | tf_op jit(solution)/shard_map/all_gather | solution.py:83
  44.9 3.0 fusion.129
  48.0 21.4 %all-reduce.1 = (f32[64]{0:T(128)S(1)}, f32[64]{0:T(128)S(1)}) all-reduce(f32[64]{0:T(128)S(1)} %get-tuple-element.4, f32[64]{0:T(128)S(1)} %get-tuple-element.3), channel_id=1, replica_groups=mesh['seq'=4,'tensor'=8] {'tensor'}, use_global_device_ids=true, to_apply=%region_4.0 | all-reduce | flops 128 | bytes 1024 | tf_op jit(solution)/shard_map/psum | solution.py:89
  69.7 2.3 copy.71
  72.1 2.3 copy.73
  74.4 1.7 maximum_bitcast_fusion
  76.6 1.0 copy-done.1
  77.6 2.9 pad_maximum_fusion
  81.4 1.3 collective-permute-start
  84.0 52.2 %all-gather.5.cloned.1.call-done = bf16[8192,2,256]{0,2,1:T(8,128)(2,1)} async-done(((bf16[2048,2,256]{0,2,1:T(8,128)(2,1)}), bf16[8192,2,256]{0,2,1:T(8,128)(2,1)}) %all-gather.5.cloned.1.call-update) | async-done | bytes 8388624 | tf_op jit(solution)/shard_map/all_gather | solution.py:174
  136.2 4.0 %fusion.123 = (bf16[2048,1,256]{0,2,1:T(8,128)(2,1)S(1)}, bf16[2048,1,256]{0,2,1:T(8,128)(2,1)S(1)}, bf16[2048,1,256]{0,2,1:T(8,128)(2,1)S(1)}, bf16[2048,1,256]...) fusion(bf16[8192,2,256]{0,2,1:T(8,128)(2,1)} %all-gather.5.clon, ...), kind=kLoop, calls=%fused_computation.176 | loop fusion | bytes 16777216 | tf_op jit(solution)/shard_map/slice | solution.py:33
  145.7 1.0 convolution_convert_fusion.1
  147.3 61.2 %reduce-scatter.3.cloned.1.call-done = bf16[8,2048]{1,0:T(8,128)(2,1)} async-done(((bf16[64,2048]{1,0:T(8,128)(2,1)}), bf16[8,2048]{1,0:T(8,128)(2,1)}) %reduce-scatter.3.cloned.1.call-update) | async-done | bytes 32784 | tf_op jit(solution)/shard_map/reduce_scatter | solution.py:194
  209.4 1.1 convolution_convert_fusion
  210.6 16.4 %all_to_all.10 = bf16[8,2,8,2048]{3,2,1,0:T(8,128)(2,1)} all-to-all(bf16[8,2,8,2048]{3,2,1,0:T(8,128)(2,1)S(1)} %bitcast.242), channel_id=1, replica_groups=mesh['seq'=4,'tensor'=8] {'tensor'}, dimensions={0} | all-to-all | bytes 1048576 | tf_op jit(solution)/shard_map/all_to_all | solution.py:222
  227.2 21.5 %all-gather.7.cloned.1.call-done = bf16[32,2,8,2048]{3,2,1,0:T(8,128)(2,1)} async-done(((bf16[8,2,8,2048]{3,2,1,0:T(8,128)(2,1)}), bf16[32,2,8,2048]{3,2,1,0:T(8,128)(2,1)}) %all-gather.7.cloned.1.call-update) | async-done | bytes 2097168 | tf_op jit(solution)/shard_map/all_gather | solution.py:228
  248.7 3.4 %fusion.9 = f32[4,8,8,512]{3,2,1,0:T(8,128)} fusion(bf16[1,2048,512]{2,1,0:T(8,128)(2,1)} %param.31, bf16[4,8,2,8,2048]{4,3,2,1,0:T(8,128)(2,1)} %bitcast.246, s32[]{:T(128)S(6)} %select_n.80), kind=kOutput, calls=%fused_computation.18 | convolution fusion | flops 536870912 | bytes 3670020 | tf_op jit(solution)/shard_map/srcd,df->srcf/dot_general | solution.py:230
  252.2 3.3 %fusion.5 = bf16[4,8,8,2048]{3,2,1,0:T(8,128)(2,1)S(1)} fusion(bf16[1,512,2048]{2,1,0:T(8,128)(2,1)S(1)} %copy-done, bf16[1,2048,512]{2,1,0:T(8,128)(2,1)} %param.32, bf16[4,8,2,8,2048]{4,3,2,1,0:T(8,128)(2,1)} %bitcast.247, s32[]{:T(128)S(6)} %select_n.80, f32[4,8,8,512]{3,2,1,0:T(8,128)} %fusion.9), kind=kOutput, calls=%fused_computation.14 | convolution fusion | flops 1074528256 | bytes 6815748 | tf_op jit(solution)/shard_map/srcf,fd->srcd/dot_general | solution.py:233
  255.5 2.0 select_convert_fusion
  257.5 31.6 %reduce-scatter.5.cloned.1.call-done = bf16[1,8,2,8,2048]{4,3,2,1,0:T(8,128)(2,1)} async-done(((bf16[4,8,2,8,2048]{4,3,2,1,0:T(8,128)(2,1)}), bf16[1,8,2,8,2048]{4,3,2,1,0:T(8,128)(2,1)}) %reduce-scatter.5.cloned.1.call-update) | async-done | bytes 524304 | tf_op jit(solution)/shard_map/reduce_scatter | solution.py:235
  289.1 5.5 %all-to-all-start.1 = ((bf16[8,2,8,2048]{3,2,1,0:T(8,128)(2,1)}), bf16[8,2,8,2048]{3,2,1,0:T(8,128)(2,1)S(1)}, u32[]{:S(2)}, u32[]{:S(2)}) async-start(bf16[8,2,8,2048]{3,2,1,0:T(8,128)(2,1)} %bitcast.243), calls=%async_computation.3 | async-start | bytes 1048576 | tf_op jit(solution)/shard_map/all_to_all | solution.py:238
  294.7 14.4 %all-to-all-done.1 = bf16[8,2,8,2048]{3,2,1,0:T(8,128)(2,1)S(1)} async-done(((bf16[8,2,8,2048]{3,2,1,0:T(8,128)(2,1)}), bf16[8,2,8,2048]{3,2,1,0:T(8,128)(2,1)S(1)}, u32[]{:S(2)}, u32[]{:S(2)}) %all-to-all-start.1) | async-done | bytes 524320 | tf_op jit(solution)/shard_map/all_to_all | solution.py:238
  309.1 0.9 fusion.4
  (94 shorter events, 10.6 us)
Async XLA Ops:
  7.2 245.0 %copy-start = (bf16[1,512,2048]{2,1,0:T(8,128)(2,1)S(1)}, bf16[1,512,2048]{2,1,0:T(8,128)(2,1)}, u32[]{:S(2)}) copy-start(bf16[1,512,2048]{2,1,0:T(8,128)(2,1)} %param.33) | copy-start | bytes 6291460
  7.2 4.9 %copy-start.9 = (bf16[2048]{0:T(1024)(128)(2,1)S(1)}, bf16[2048]{0:T(1024)(128)(2,1)}, u32[]{:S(2)}) copy-start(bf16[2048]{0:T(1024)(128)(2,1)} %param.18) | copy-start | bytes 12292
  7.2 4.9 %copy-start.4 = (bf16[8,2048]{1,0:T(8,128)(2,1)S(1)}, bf16[8,2048]{1,0:T(8,128)(2,1)}, u32[]{:S(2)}) copy-start(bf16[8,2048]{1,0:T(8,128)(2,1)} %param.17) | copy-start | bytes 98308
  7.2 129.0 %all-gather.5.cloned.1.call-start = ((), (), s32[]{:S(2)}) async-start(), calls=%async_computation.6 | async-start | bytes 10485760 | tf_op jit(solution)/shard_map/all_gather | solution.py:174
  12.1 35.9 %copy-start.14 = (bf16[256]{0:T(256)(128)(2,1)S(1)}, bf16[256]{0:T(256)(128)(2,1)}, u32[]{:S(2)}) copy-start(bf16[256]{0:T(256)(128)(2,1)} %param.20) | copy-start | bytes 1540
  12.1 35.9 %copy-start.15 = (bf16[256]{0:T(256)(128)(2,1)S(1)}, bf16[256]{0:T(256)(128)(2,1)}, u32[]{:S(2)}) copy-start(bf16[256]{0:T(256)(128)(2,1)} %param.21) | copy-start | bytes 1540
  48.0 26.4 %copy-start.7 = (bf16[64,256]{1,0:T(8,128)(2,1)}, bf16[64,256]{1,0:T(8,128)(2,1)S(1)}, u32[]{:S(2)}) copy-start(bf16[64,256]{1,0:T(8,128)(2,1)S(1)} %slice.115) | copy-start | bytes 98308
  69.6 4.8 %copy-start.6 = (bf16[64,256]{1,0:T(8,128)(2,1)}, bf16[64,256]{1,0:T(8,128)(2,1)S(1)}, u32[]{:S(2)}) copy-start(bf16[64,256]{1,0:T(8,128)(2,1)S(1)} %get-tuple-element.26) | copy-start | bytes 98308
  74.4 1.7 copy-start.2
  76.6 1.0 copy-start.1
  80.4 2.3 copy-start.12
  80.4 2.3 copy-start.13
  80.5 2.6 copy-start.16
  80.5 2.8 copy-start.8
  80.5 128.0 %reduce-scatter.3.cloned.1.call-start = ((), (), s32[]{:S(2)}) async-start(), calls=%async_computation.4 | async-start | bytes 294912 | tf_op jit(solution)/shard_map/reduce_scatter | solution.py:194
  81.4 2.3 collective-permute-start
  144.4 1.3 copy-start.3
  145.1 2.1 copy-start.10
  146.7 102.0 %all-gather.7.cloned.1.call-start = ((), (), s32[]{:S(2)}) async-start(), calls=%async_computation.7 | async-start | bytes 2621440 | tf_op jit(solution)/shard_map/all_gather | solution.py:228
  226.9 62.1 %reduce-scatter.5.cloned.1.call-start = ((), (), s32[]{:S(2)}) async-start(), calls=%async_computation.5 | async-start | bytes 2621440 | tf_op jit(solution)/shard_map/reduce_scatter | solution.py:235
  257.4 37.2 %copy-start.11 = (f32[8,8]{1,0:T(8,128)S(1)}, f32[8,8]{1,0:T(8,128)}, u32[]{:S(2)}) copy-start(f32[8,8]{1,0:T(8,128)} %param.30) | copy-start | bytes 772
  257.4 51.6 %copy-start.5 = (bf16[8,2048]{1,0:T(8,128)(2,1)S(1)}, bf16[8,2048]{1,0:T(8,128)(2,1)}, u32[]{:S(2)}) copy-start(bf16[8,2048]{1,0:T(8,128)(2,1)} %reduce-scatter.3.cloned.1.call-done) | copy-start | bytes 98308
  289.1 20.0 %all-to-all-start.1 = ((bf16[8,2,8,2048]{3,2,1,0:T(8,128)(2,1)}), bf16[8,2,8,2048]{3,2,1,0:T(8,128)(2,1)S(1)}, u32[]{:S(2)}, u32[]{:S(2)}) async-start(bf16[8,2,8,2048]{3,2,1,0:T(8,128)(2,1)} %bitcast.243), calls=%async_computation.3 | async-start | bytes 1048576 | tf_op jit(solution)/shard_map/all_to_all | solution.py:238
Sparse Core Ops, SparseCore 0:
  80.6 55.5 all-gather.4
  146.9 61.6 reduce-scatter.2
  227.1 21.6 all-gather.6
  257.6 31.4 reduce-scatter.4
where the time goes:
time: 317 us
  waiting for transfers between devices  181 us (57%)
  blocking collectives  70.3 us (22%)
  matrix products  16.9 us (5%)
  local copies, waits for them, and re-layouts  15 us (5%)
  between operations  14.1 us (4%)
  other arithmetic  11.7 us (4%)
  starting transfers between devices  7.16 us (2%)
    reduce_scatter x1, waiting for transfers between devices, local(): lax.psum_scatter(jnp.dot(attended_local, w_out, preferred_element_type=jn...  61.2 us
    all_gather x1, waiting for transfers between devices, local(): piece = lax.all_gather(prefix_full[None], 'seq', axis=0, tiled=True)  52.2 us
    all_gather x1, blocking collectives, local(): lax.all_gather(normed, 'tensor', axis=0, tiled=True)  32.5 us
    reduce_scatter x1, waiting for transfers between devices, local(): lax.psum_scatter(partials.astype(jnp.bfloat16), 'seq', scatter_dimension=...  31.6 us
    all_gather x1, waiting for transfers between devices, local(): lax.all_gather(received[None], 'seq', axis=0, tiled=True)  21.5 us
    psum x1, blocking collectives, local(): lax.psum((jnp.sum(query_part * query_part, axis=-1), jnp.sum(key_part * k...  21.4 us
    all_to_all x1, blocking collectives, local(): lax.all_to_all(buffer, 'tensor', split_axis=0, concat_axis=0, tiled=True)  16.4 us
    all_to_all x1, waiting for transfers between devices, local(): lax.all_to_all(summed[0].astype(jnp.bfloat16), 'tensor', split_axis=0, co...  14.4 us
  transfers between devices with their start and end apart: 6, of which 6 were waited for; matrix products, arithmetic and copies ran while one was open for 1% of the time, Pallas kernels for 0%

commit v1 on v0

--- a/solution.py
+++ b/solution.py
@@ -1,6 +1,10 @@
+import functools
+
 import jax
 import jax.numpy as jnp
 from jax import lax
+from jax.experimental import pallas as pl
+from jax.experimental.pallas import tpu as pltpu
 from jax.sharding import PartitionSpec as P
 
 HD = 128
@@ -248,9 +252,369 @@
     return (output, new_keys, new_values)
 
 
+MESH = pl.DeviceIdType.MESH
+F32 = jnp.float32
+BF16 = jnp.bfloat16
+
+
+def pack_rows(value):
+    half = value.shape[-1] // 2
+    return jnp.concatenate([value[:, :, :half], value[:, :, half:]], axis=1).astype(BF16)
+
+
+def unpack_rows(value):
+    count, rows, half = value.shape
+    wide = value.astype(F32).reshape(count, 2, rows // 2, half)
+    left = wide[:, 0].reshape(count * (rows // 2), half)
+    right = wide[:, 1].reshape(count * (rows // 2), half)
+    return jnp.concatenate([left, right], axis=-1)
+
+
+def layer_kernel(
+    dims,
+    tokens_ref, attn_gain_ref, q_gain_ref, k_gain_ref, mlp_gain_ref,
+    seg_row_ref, cols_ref, ids_ref, gates_ref,
+    wqkv_hbm, wout_hbm, pk_hbm, pv_hbm, wg_hbm, wu_hbm, wd_hbm,
+    out_ref, keys_ref, values_ref,
+    wqkv, wout, pk, pv, wg, wu, wd,
+    ag, sq, qkv, att_snd, att_in, rs_snd, rs_in,
+    grid_a, grid_b, gate_grid,
+    res_a, res_b, rc_a, rc_b, s1_a, s1_b, r1_a, r1_b,
+    s2_a, s2_b, r2_a, r2_b, s3_a, s3_b, r3_a, r3_b,
+    w_sem,
+    ag_ss, ag_rs, sq_ss, sq_rs, qkv_ss, qkv_rs, att_ss, att_rs, rs_ss, rs_rs,
+    gg_ss, gg_rs, ga_ss, ga_rs, gb_ss, gb_rs, ra_ss, ra_rs, rb_ss, rb_rs,
+):
+    S, T, NZ, exp_local = dims
+    s = lax.axis_index("seq")
+    t = lax.axis_index("tensor")
+    x, c = s // 2, s % 2
+    z, y = t // 2, t % 2
+    tok, width = tokens_ref.shape
+    cols = keys_ref.shape[1]
+    tok_seq = tok * T
+    total_tok = tok_seq * S
+    started = []
+
+    loads = [
+        pltpu.make_async_copy(wqkv_hbm, wqkv, w_sem.at[0]),
+        pltpu.make_async_copy(pk_hbm.at[0], pk, w_sem.at[1]),
+        pltpu.make_async_copy(pv_hbm.at[0], pv, w_sem.at[2]),
+        pltpu.make_async_copy(wout_hbm, wout, w_sem.at[3]),
+        pltpu.make_async_copy(wg_hbm.at[0], wg, w_sem.at[4]),
+        pltpu.make_async_copy(wu_hbm.at[0], wu, w_sem.at[5]),
+        pltpu.make_async_copy(wd_hbm.at[0], wd, w_sem.at[6]),
+    ]
+    for load in loads:
+        load.start()
+
+    barrier = pltpu.get_barrier_semaphore()
+    for k in range(1, T):
+        pl.semaphore_signal(barrier, inc=1, device_id=(s, (t + k) % T), device_id_type=MESH)
+    for k in range(1, S):
+        pl.semaphore_signal(barrier, inc=1, device_id=((s + k) % S, t), device_id_type=MESH)
+
+    def send(src, dst, send_sem, recv_sem, to):
+        copy = pltpu.make_async_remote_copy(
+            src_ref=src, dst_ref=dst, send_sem=send_sem, recv_sem=recv_sem,
+            device_id=to, device_id_type=MESH,
+        )
+        copy.start()
+        started.append(copy)
+        return copy
+
+    def to_tensor(k):
+        return (s, (t + k) % T)
+
+    def to_seq(k):
+        return ((s + k) % S, t)
+
+    peer_x = ((1 - x) * 2 + c, t)
+    peer_c = (x * 2 + 1 - c, t)
+    peer_y = (s, z * 2 + 1 - y)
+
+    def to_z(k):
+        return (s, ((z + k) % NZ) * 2 + y)
+
+    def rms(value, gain):
+        mean_square = jnp.mean(value * value, axis=-1, keepdims=True)
+        return value * lax.rsqrt(mean_square + 1e-05) * gain
+
+    tokens = tokens_ref[...].astype(F32)
+    normed = rms(tokens, attn_gain_ref[...].astype(F32))
+    ag[t] = pack_rows(normed[None])[0]
+    lane = lax.broadcasted_iota(jnp.int32, (tok, 128), 1)
+    dense = jnp.zeros((tok, 128), F32)
+    for k in range(ids_ref.shape[1]):
+        dense = dense + jnp.where(ids_ref[:, k : k + 1] == lane, gates_ref[:, k : k + 1], 0.0)
+    gate_grid[c, x, y, z] = dense
+    pl.semaphore_wait(barrier, T + S - 2)
+    ag_copies = [
+        send(ag.at[t], ag.at[t], ag_ss.at[k], ag_rs.at[k], to_tensor(k)) for k in range(1, T)
+    ]
+    gg_z = [
+        send(gate_grid.at[c, x, y, z], gate_grid.at[c, x, y, z], gg_ss.at[k], gg_rs.at[k], to_z(k))
+        for k in range(1, NZ)
+    ]
+    for copy in ag_copies:
+        copy.wait_recv()
+    rows = unpack_rows(ag[...]).astype(BF16)
+    loads[0].wait()
+    proj_q = jnp.dot(rows, wqkv[0], preferred_element_type=F32)
+    proj_k = jnp.dot(rows, wqkv[1], preferred_element_type=F32)
+
+    ones = jnp.ones((8, cols), F32)
+    nt = (((1,), (1,)), ((), ()))
+    squares = jnp.concatenate([proj_q * proj_q, proj_k * proj_k], axis=0)
+    sq[t] = lax.dot_general(
+        ones, squares, nt, precision=lax.Precision.HIGHEST, preferred_element_type=F32
+    )
+    sq_copies = [
+        send(sq.at[t], sq.at[t], sq_ss.at[k], sq_rs.at[k], to_tensor(k)) for k in range(1, T)
+    ]
+    for copy in gg_z:
+        copy.wait_recv()
+    gg_y = send(gate_grid.at[c, x, y], gate_grid.at[c, x, y], gg_ss.at[4], gg_rs.at[4], peer_y)
+    proj_v = jnp.dot(rows, wqkv[2], preferred_element_type=F32).astype(BF16)
+    values_ref[...] = proj_v
+    qkv[s, 2 * tok_seq :] = proj_v
+    for copy in sq_copies:
+        copy.wait_recv()
+    sums = lax.dot_general(
+        sq[...].reshape(8 * T, 2 * tok_seq), jnp.full((8 * T, cols), 0.125, F32),
+        (((0,), (0,)), ((), ())), precision=lax.Precision.HIGHEST, preferred_element_type=F32,
+    )
+    inverse = lax.rsqrt(sums / width + 1e-05)
+    new_q = (proj_q * inverse[:tok_seq] * q_gain_ref[...].astype(F32)).astype(BF16)
+    new_k = (proj_k * inverse[tok_seq:] * k_gain_ref[...].astype(F32)).astype(BF16)
+    keys_ref[...] = new_k
+    qkv[s, :tok_seq] = new_q
+    qkv[s, tok_seq : 2 * tok_seq] = new_k
+    qkv_copies = [
+        send(qkv.at[s], qkv.at[s], qkv_ss.at[k], qkv_rs.at[k], to_seq(k)) for k in range(1, S)
+    ]
+    gg_y.wait_recv()
+    gg_x = send(gate_grid.at[c, x], gate_grid.at[c, x], gg_ss.at[5], gg_rs.at[5], peer_x)
+    for copy in qkv_copies:
+        copy.wait_recv()
+    loads[1].wait()
+    loads[2].wait()
+
+    all_q = qkv[:, :tok_seq].reshape(total_tok, cols)
+    all_k = qkv[:, tok_seq : 2 * tok_seq].reshape(total_tok, cols)
+    all_v = qkv[:, 2 * tok_seq :].reshape(total_tok, cols)
+    pos_q = lax.broadcasted_iota(jnp.int32, (total_tok, total_tok), 0)
+    pos_k = lax.broadcasted_iota(jnp.int32, (total_tok, total_tok), 1)
+    mask = (cols_ref[:, 0:1] == seg_row_ref[...]) & (pos_k <= pos_q)
+    mine = cols_ref[:, 1:2] == s
+    heads = []
+    for h in range(cols // HD):
+        part = slice(h * HD, (h + 1) * HD)
+        q_h = all_q[:, part]
+        pre = lax.dot_general(q_h, pk[:, part], nt, preferred_element_type=F32) * HD ** (-0.5)
+        suf = lax.dot_general(q_h, all_k[:, part], nt, preferred_element_type=F32) * HD ** (-0.5)
+        suf = jnp.where(mask, suf, -1e30)
+        top = jnp.maximum(
+            jnp.max(pre, axis=-1, keepdims=True), jnp.max(suf, axis=-1, keepdims=True)
+        )
+        pre = jnp.exp(pre - top)
+        suf = jnp.where(mask, jnp.exp(suf - top), 0.0)
+        total = jnp.sum(pre, axis=-1, keepdims=True) + jnp.sum(suf, axis=-1, keepdims=True)
+        mix = jnp.dot(pre.astype(BF16), pv[:, part], preferred_element_type=F32)
+        mix = mix + jnp.dot(suf.astype(BF16), all_v[:, part], preferred_element_type=F32)
+        heads.append(jnp.where(mine, mix / total, 0.0).astype(BF16))
+    att_snd[...] = jnp.concatenate(heads, axis=-1).reshape(S, tok_seq, cols)
+    att_copies = [
+        send(att_snd.at[(s + k) % S], att_in.at[k], att_ss.at[k], att_rs.at[k], to_seq(k))
+        for k in range(1, S)
+    ]
+    gg_x.wait_recv()
+    gg_c = send(gate_grid.at[c], gate_grid.at[c], gg_ss.at[6], gg_rs.at[6], peer_c)
+    attended = att_snd[s].astype(F32)
+    for k in range(1, S):
+        att_copies[k - 1].wait_recv()
+        attended = attended + att_in[k].astype(F32)
+    loads[3].wait()
+    partial = jnp.dot(attended.astype(BF16), wout[...], preferred_element_type=F32)
+    rs_snd[...] = pack_rows(partial.reshape(T, tok, width))
+    rs_copies = [
+        send(rs_snd.at[(t + k) % T], rs_in.at[k], rs_ss.at[k], rs_rs.at[k], to_tensor(k))
+        for k in range(1, T)
+    ]
+    attn_sum = rs_snd[t].astype(F32)
+    for k in range(1, T):
+        rs_copies[k - 1].wait_recv()
+        attn_sum = attn_sum + rs_in[k].astype(F32)
+    attn_sum = jnp.concatenate([attn_sum[:tok], attn_sum[tok:]], axis=-1)
+    mixed = (tokens + attn_sum).astype(BF16).astype(F32)
+    expert_in = rms(mixed, mlp_gain_ref[...].astype(F32))
+
+    half = width // 2
+    grid_a[c, x, y, z] = pack_rows(expert_in[None, :, :half])[0]
+    grid_b[c, y, x, z] = pack_rows(expert_in[None, :, half:])[0]
+    mine_a, mine_b = grid_a.at[c, x, y, z], grid_b.at[c, y, x, z]
+    z_a = [send(mine_a, mine_a, ga_ss.at[k], ga_rs.at[k], to_z(k)) for k in range(1, NZ)]
+    z_b = [send(mine_b, mine_b, gb_ss.at[k], gb_rs.at[k], to_z(k)) for k in range(1, NZ)]
+    for copy in z_a:
+        copy.wait_recv()
+    two_a = send(grid_a.at[c, x, y], grid_a.at[c, x, y], ga_ss.at[4], ga_rs.at[4], peer_y)
+    for copy in z_b:
+        copy.wait_recv()
+    two_b = send(grid_b.at[c, y, x], grid_b.at[c, y, x], gb_ss.at[4], gb_rs.at[4], peer_x)
+    two_a.wait_recv()
+    one_a = send(grid_a.at[c, x], grid_a.at[c, x], ga_ss.at[5], ga_rs.at[5], peer_x)
+    two_b.wait_recv()
+    one_b = send(grid_b.at[c, y], grid_b.at[c, y], gb_ss.at[5], gb_rs.at[5], peer_y)
+    one_a.wait_recv()
+    core_a = send(grid_a.at[c], grid_a.at[c], ga_ss.at[6], ga_rs.at[6], peer_c)
+    one_b.wait_recv()
+    core_b = send(grid_b.at[c], grid_b.at[c], gb_ss.at[6], gb_rs.at[6], peer_c)
+    for load in loads[4:]:
+        load.wait()
+    gg_c.wait_recv()
+    expert = exp_local * t + s // (S // exp_local)
+    blocks = 4 * NZ
+
+    def run_half(side):
+        block_a = grid_a[side].reshape(blocks, 2 * tok, half // 2)
+        raw_b = grid_b[side]
+        block_b = jnp.concatenate([raw_b[j, i] for i in range(2) for j in range(2)], axis=0)
+        inputs = jnp.concatenate([unpack_rows(block_a), unpack_rows(block_b)], axis=-1).astype(BF16)
+        gated = jnp.dot(inputs, wg[...], preferred_element_type=F32)
+        upward = jnp.dot(inputs, wu[...], preferred_element_type=F32)
+        act = (gated / (1.0 + jnp.exp(-gated)) * upward).astype(BF16)
+        result = jnp.dot(act, wd[...], preferred_element_type=F32)
+        table = gate_grid[side].reshape(blocks * tok, 128)
+        lanes = lax.broadcasted_iota(jnp.int32, table.shape, 1)
+        scale = jnp.sum(jnp.where(lanes == expert, table, 0.0), axis=-1, keepdims=True)
+        result = (result * scale).reshape(blocks, tok, width)
+        res_a[side] = pack_rows(result[:, :, :half]).reshape(2, 2, NZ, 2 * tok, half // 2)
+        packed_b = pack_rows(result[:, :, half:])
+        for i in range(2):
+            for j in range(2):
+                first = (i * 2 + j) * NZ
+                res_b[side, j, i] = packed_b[first : first + NZ]
+
+    core_a.wait_recv()
+    core_b.wait_recv()
+    run_half(1 - c)
+    rcore_a = send(res_a.at[1 - c], rc_a, ra_ss.at[0], ra_rs.at[0], peer_c)
+    rcore_b = send(res_b.at[1 - c], rc_b, rb_ss.at[0], rb_rs.at[0], peer_c)
+    run_half(c)
+
+    def added(first, second):
+        return (first.astype(F32) + second.astype(F32)).astype(BF16)
+
+    rcore_a.wait_recv()
+    s1_a[...] = added(res_a[c], rc_a[...])
+    rone_a = send(s1_a.at[1 - x], r1_a, ra_ss.at[1], ra_rs.at[1], peer_x)
+    rcore_b.wait_recv()
+    s1_b[...] = added(res_b[c], rc_b[...])
+    rone_b = send(s1_b.at[1 - y], r1_b, rb_ss.at[1], rb_rs.at[1], peer_y)
+    rone_b.wait_recv()
+    s2_b[...] = added(s1_b[y], r1_b[...])
+    rone_a.wait_recv()
+    s2_a[...] = added(s1_a[x], r1_a[...])
+    rtwo_a = send(s2_a.at[1 - y], r2_a, ra_ss.at[2], ra_rs.at[2], peer_y)
+    rtwo_b = send(s2_b.at[1 - x], r2_b, rb_ss.at[2], rb_rs.at[2], peer_x)
+    rtwo_a.wait_recv()
+    s3_a[...] = added(s2_a[y], r2_a[...])
+    rz_a = [
+        send(s3_a.at[(z + k) % NZ], r3_a.at[k], ra_ss.at[2 + k], ra_rs.at[2 + k], to_z(k))
+        for k in range(1, NZ)
+    ]
+    rtwo_b.wait_recv()
+    s3_b[...] = added(s2_b[x], r2_b[...])
+    rz_b = [
+        send(s3_b.at[(z + k) % NZ], r3_b.at[k], rb_ss.at[2 + k], rb_rs.at[2 + k], to_z(k))
+        for k in range(1, NZ)
+    ]
+    sum_a = s3_a[z].astype(F32)
+    sum_b = s3_b[z].astype(F32)
+    for k in range(1, NZ):
+        rz_a[k - 1].wait_recv()
+        sum_a = sum_a + r3_a[k].astype(F32)
+    for k in range(1, NZ):
+        rz_b[k - 1].wait_recv()
+        sum_b = sum_b + r3_b[k].astype(F32)
+    moe = jnp.concatenate([sum_a[:tok], sum_a[tok:], sum_b[:tok], sum_b[tok:]], axis=-1)
+    out_ref[...] = (mixed + moe).astype(BF16)
+    for copy in started:
+        copy.wait_send()
+
+
+def local_kernel(
+    tokens, attn_gain, w_qkv, q_gain, k_gain, w_out, prefix_keys, prefix_values, segments,
+    request_group, prefix_owner, mlp_gain, expert_ids, gate_weights, w_gate, w_up, w_down,
+):
+    S, T = lax.axis_size("seq"), lax.axis_size("tensor")
+    NZ = T // 2
+    tok, width = tokens.shape
+    cols = w_qkv.shape[2]
+    tok_seq = tok * T
+    slots = prefix_keys.shape[1]
+    units = w_gate.shape[2]
+    request = jnp.arange(request_group.shape[0], dtype=jnp.int32)
+    group = jnp.arange(prefix_owner.shape[0], dtype=jnp.int32)
+    owner_of_request = jnp.sum(
+        jnp.where(request_group[:, None] == group[None, :], prefix_owner[None, :], 0), axis=1
+    )
+    owner = jnp.sum(
+        jnp.where(segments[:, None] == request[None, :], owner_of_request[None, :], 0), axis=1
+    )
+    columns = jnp.stack([segments, owner], axis=1)
+    vm, dma = pltpu.VMEM, pltpu.SemaphoreType.DMA
+    quarter = width // 4
+    blk = (2 * tok, quarter)
+    grid = vm((2, 2, 2, NZ) + blk, BF16)
+    pair = lambda *lead: [vm(lead + blk, BF16)] * 2
+    scratch = [
+        vm((3, width, cols), BF16), vm((cols, width), BF16),
+        vm((slots, cols), BF16), vm((slots, cols), BF16),
+        vm((width, units), BF16), vm((width, units), BF16), vm((units, width), BF16),
+        vm((T, 2 * tok, width // 2), BF16), vm((T, 8, 2 * tok_seq), F32),
+        vm((S, 3 * tok_seq, cols), BF16), vm((S, tok_seq, cols), BF16), vm((S, tok_seq, cols), BF16),
+        vm((T, 2 * tok, width // 2), BF16), vm((T, 2 * tok, width // 2), BF16),
+        grid, grid, vm((2, 2, 2, NZ, tok, 128), F32),
+        grid, grid,
+        *pair(2, 2, NZ), *pair(2, 2, NZ), *pair(2, NZ),
+        *pair(2, NZ), *pair(NZ), *pair(NZ), *pair(NZ),
+        dma((7,)),
+        *[dma((T,))] * 4, *[dma((S,))] * 4, *[dma((T,))] * 2,
+        *[dma((8,))] * 10,
+    ]
+    in_vmem = pl.BlockSpec(memory_space=pltpu.VMEM)
+    in_any = pl.BlockSpec(memory_space=pl.ANY)
+    return pl.pallas_call(
+        functools.partial(layer_kernel, (S, T, NZ, EXP_DEV)),
+        out_shape=(
+            jax.ShapeDtypeStruct((tok, width), BF16),
+            jax.ShapeDtypeStruct((tok_seq, cols), BF16),
+            jax.ShapeDtypeStruct((tok_seq, cols), BF16),
+        ),
+        in_specs=[in_vmem] * 9 + [in_any] * 7,
+        out_specs=(in_vmem,) * 3,
+        scratch_shapes=scratch,
+        compiler_params=pltpu.CompilerParams(
+            collective_id=0, has_side_effects=True, vmem_limit_bytes=56 * 2**20
+        ),
+    )(
+        tokens, attn_gain[None], q_gain[None], k_gain[None], mlp_gain[None],
+        segments[None], columns, expert_ids, gate_weights,
+        jnp.transpose(w_qkv, (1, 0, 2)), w_out, prefix_keys, prefix_values, w_gate, w_up, w_down,
+    )
+
+
+def whole_heads(*arrays):
+    seq_size, tensor_size = lax.axis_size("seq"), lax.axis_size("tensor")
+    if arrays[2].shape[2] % HD == 0 and seq_size == 4 and tensor_size == 8:
+        return local_kernel(*arrays)
+    return local(*arrays)
+
+
 def solution(mesh):
     return jax.shard_map(
-        local,
+        whole_heads,
         mesh=mesh,
         in_specs=(
             P(("seq", "tensor"), None),

time: 317 us -> 81.7 us (0.26)
  waiting for transfers between devices: 181 us -> 0 us
  blocking collectives: 70.3 us -> 0 us
  Pallas kernels: 0 us -> 68.5 us
  matrix products: 16.9 us -> 0 us
  between operations: 14.1 us -> 0.64 us
  other arithmetic: 11.7 us -> 2.21 us
  starting transfers between devices: 7.16 us -> 0 us
  local copies, waits for them, and re-layouts: 15 us -> 9.9 us
    reduce_scatter x2 -> x0, waiting for transfers between devices: 92.8 us -> none  [the longest x1 61.2 us: local(): lax.psum_scatter(jnp.dot(attended_local, w_out, preferred_element_type=jn...]
    all_gather x2 -> x0, waiting for transfers between devices: 73.8 us -> none  [the longest x1 52.2 us: local(): piece = lax.all_gather(prefix_full[None], 'seq', axis=0, tiled=True)]
    pallas_call x0 -> x1, Pallas kernels: none -> 68.5 us  [local_kernel(): pl.pallas_call(functools.partial(layer_kernel, (S, T, NZ, EXP_DEV)), out_...]
    all_gather x1 -> x0, blocking collectives: 32.5 us -> none  [local(): lax.all_gather(normed, 'tensor', axis=0, tiled=True)]
    psum x1 -> x0, blocking collectives: 21.4 us -> none  [local(): lax.psum((jnp.sum(query_part * query_part, axis=-1), jnp.sum(key_part * k...]
    dot_general x16 -> x0, matrix products: 16.9 us -> none  [the longest x1 3.42 us: local(): jnp.einsum('srcd,df->srcf', chosen, gate_local, preferred_element_type=jn...]
    all_to_all x1 -> x0, blocking collectives: 16.4 us -> none  [local(): lax.all_to_all(buffer, 'tensor', split_axis=0, concat_axis=0, tiled=True)]
    all_to_all x1 -> x0, waiting for transfers between devices: 14.4 us -> none  [local(): lax.all_to_all(summed[0].astype(jnp.bfloat16), 'tensor', split_axis=0, co...]
  transfers between devices with their start and end apart: 6 -> 0, of which waited for: 6 -> 0; matrix products, arithmetic and copies ran while one was open for 1% -> 0% of each run, Pallas kernels for 0% -> 0%
where the time goes in v1:
time: 81.7 us; the launch traced here: 81.2 us
  Pallas kernels  68.5 us (84%)
  local copies, waits for them, and re-layouts  9.9 us (12%)
  other arithmetic  2.21 us (3%)
    pallas_call x1, Pallas kernels, local_kernel(): pl.pallas_call(functools.partial(layer_kernel, (S, T, NZ, EXP_DEV)), out_...  68.5 us
    unnamed x3, local copies, waits for them, and re-layouts  4.12 us

profile of v1, /device:TPU:0, one launch (start us, length us, event | category | flops | bytes accessed | tf_op | source)
XLA Modules:
  0.0 81.2 jit_solution(1700875957904935350)
XLA Ops:
  0.6 0.8 fusion
  1.4 0.8 select_reduce_fusion
  2.2 0.7 pad_add_fusion
  2.8 1.2 %broadcast_in_dim.46.q_gain_ref = bf16[1,256]{1,0:T(2,128)(2,1)} reshape(bf16[256]{0:T(256)(128)(2,1)} %param.20) | data formatting | bytes 1024 | tf_op jit(solution)/shard_map/broadcast_in_dim | solution.py:602
  4.1 1.2 %broadcast_in_dim.47.k_gain_ref = bf16[1,256]{1,0:T(2,128)(2,1)} reshape(bf16[256]{0:T(256)(128)(2,1)} %param.21) | data formatting | bytes 1024 | tf_op jit(solution)/shard_map/broadcast_in_dim | solution.py:602
  5.3 1.3 %broadcast_in_dim.45.attn_gain_ref = bf16[1,2048]{1,0:T(2,128)(2,1)} reshape(bf16[2048]{0:T(1024)(128)(2,1)} %param.18) | data formatting | bytes 8192 | tf_op jit(solution)/shard_map/broadcast_in_dim | solution.py:602
  6.5 1.3 %broadcast_in_dim.48.mlp_gain_ref = bf16[1,2048]{1,0:T(2,128)(2,1)} reshape(bf16[2048]{0:T(1024)(128)(2,1)} %param.28) | data formatting | bytes 8192 | tf_op jit(solution)/shard_map/broadcast_in_dim | solution.py:602
  7.8 0.8 copy.23.cols_ref
  8.6 68.5 %shard_map.184 = (bf16[8,2048]{1,0:T(8,128)(2,1)}, bf16[64,256]{1,0:T(8,128)(2,1)}, bf16[64,256]{1,0:T(8,128)(2,1)}) custom-call(bf16[8,2048]{1,0:T(8,128)(2,1)} %tokens_ref.1, bf16[1,2048]{1,0:T(2,128)(2,1)} %broadcast_in_dim.45.attn_gain_ref, bf16[1,256]{1,0:T(2,128)(2,1)} %broadcast_in_dim.46.q_gain_ref, bf16[1,256]{1,0:T(2,128)(2,1)} %broadcast_in_dim.47.k_gain_ref, ...), custom_call_target="tpu_custom_call" | custom-call | tf_op jit(solution)/shard_map/pallas_call | solution.py:588
  77.1 1.4 %copy.27 = bf16[8,2048]{1,0:T(8,128)(2,1)} copy(bf16[8,2048]{1,0:T(8,128)(2,1)} %get-tuple-element.6) | data formatting | bytes 65536
  78.5 1.4 %copy.28 = bf16[64,256]{1,0:T(8,128)(2,1)} copy(bf16[64,256]{1,0:T(8,128)(2,1)} %get-tuple-element.7) | data formatting | bytes 65536
  79.9 1.4 %copy.29 = bf16[64,256]{1,0:T(8,128)(2,1)} copy(bf16[64,256]{1,0:T(8,128)(2,1)} %get-tuple-element.8) | data formatting | bytes 65536

commit v2 on v1

--- a/solution.py
+++ b/solution.py
@@ -273,16 +273,16 @@
 def layer_kernel(
     dims,
     tokens_ref, attn_gain_ref, q_gain_ref, k_gain_ref, mlp_gain_ref,
-    seg_row_ref, cols_ref, ids_ref, gates_ref,
+    seg_row_ref, request_ref, slot_ref, ids_ref, gates_ref,
     wqkv_hbm, wout_hbm, pk_hbm, pv_hbm, wg_hbm, wu_hbm, wd_hbm,
     out_ref, keys_ref, values_ref,
     wqkv, wout, pk, pv, wg, wu, wd,
-    ag, sq, qkv, att_snd, att_in, rs_snd, rs_in,
+    ag, sq, sums_grid, qv, ks, att_snd, att_in, rs_snd, rs_in,
     grid_a, grid_b, gate_grid,
     res_a, res_b, rc_a, rc_b, s1_a, s1_b, r1_a, r1_b,
     s2_a, s2_b, r2_a, r2_b, s3_a, s3_b, r3_a, r3_b,
     w_sem,
-    ag_ss, ag_rs, sq_ss, sq_rs, qkv_ss, qkv_rs, att_ss, att_rs, rs_ss, rs_rs,
+    ag_ss, ag_rs, sq_ss, sq_rs, qv_ss, qv_rs, ks_ss, ks_rs, sm_ss, sm_rs, att_ss, att_rs, rs_ss, rs_rs,
     gg_ss, gg_rs, ga_ss, ga_rs, gb_ss, gb_rs, ra_ss, ra_rs, rb_ss, rb_rs,
 ):
     S, T, NZ, exp_local = dims
@@ -341,7 +341,7 @@
         return value * lax.rsqrt(mean_square + 1e-05) * gain
 
     tokens = tokens_ref[...].astype(F32)
-    normed = rms(tokens, attn_gain_ref[...].astype(F32))
+    normed = rms(tokens, attn_gain_ref[...].astype(F32).reshape(1, width))
     ag[t] = pack_rows(normed[None])[0]
     lane = lax.broadcasted_iota(jnp.int32, (tok, 128), 1)
     dense = jnp.zeros((tok, 128), F32)
@@ -377,42 +377,67 @@
     gg_y = send(gate_grid.at[c, x, y], gate_grid.at[c, x, y], gg_ss.at[4], gg_rs.at[4], peer_y)
     proj_v = jnp.dot(rows, wqkv[2], preferred_element_type=F32).astype(BF16)
     values_ref[...] = proj_v
-    qkv[s, 2 * tok_seq :] = proj_v
+    qv[s, :tok_seq] = (proj_q * q_gain_ref[...].astype(F32).reshape(1, cols)).astype(BF16)
+    qv[s, tok_seq:] = proj_v
+    qv_copies = [send(qv.at[s], qv.at[s], qv_ss.at[k], qv_rs.at[k], to_seq(k)) for k in range(1, S)]
     for copy in sq_copies:
         copy.wait_recv()
-    sums = lax.dot_general(
-        sq[...].reshape(8 * T, 2 * tok_seq), jnp.full((8 * T, cols), 0.125, F32),
-        (((0,), (0,)), ((), ())), precision=lax.Precision.HIGHEST, preferred_element_type=F32,
-    )
-    inverse = lax.rsqrt(sums / width + 1e-05)
-    new_q = (proj_q * inverse[:tok_seq] * q_gain_ref[...].astype(F32)).astype(BF16)
-    new_k = (proj_k * inverse[tok_seq:] * k_gain_ref[...].astype(F32)).astype(BF16)
+    sums_row = sq[0]
+    for k in range(1, T):
+        sums_row = sums_row + sq[k]
+    sums_grid[s] = sums_row
+    sums_copies = [
+        send(sums_grid.at[s], sums_grid.at[s], sm_ss.at[k], sm_rs.at[k], to_seq(k))
+        for k in range(1, S)
+    ]
+
+    def inverse_columns(sums):
+        turned = lax.dot_general(
+            sums, jnp.full((8, 128), 0.125, F32), (((0,), (0,)), ((), ())),
+            precision=lax.Precision.HIGHEST, preferred_element_type=F32,
+        )
+        return lax.rsqrt(turned / width + 1e-05)[:, :1]
+
+    new_k = (
+        proj_k * inverse_columns(sums_row)[tok_seq:] * k_gain_ref[...].astype(F32).reshape(1, cols)
+    ).astype(BF16)
     keys_ref[...] = new_k
-    qkv[s, :tok_seq] = new_q
-    qkv[s, tok_seq : 2 * tok_seq] = new_k
-    qkv_copies = [
-        send(qkv.at[s], qkv.at[s], qkv_ss.at[k], qkv_rs.at[k], to_seq(k)) for k in range(1, S)
-    ]
+    ks[s] = new_k
+    ks_copies = [send(ks.at[s], ks.at[s], ks_ss.at[k], ks_rs.at[k], to_seq(k)) for k in range(1, S)]
     gg_y.wait_recv()
     gg_x = send(gate_grid.at[c, x], gate_grid.at[c, x], gg_ss.at[5], gg_rs.at[5], peer_x)
-    for copy in qkv_copies:
-        copy.wait_recv()
+    pos_q = lax.broadcasted_iota(jnp.int32, (total_tok, total_tok), 0)
+    pos_k = lax.broadcasted_iota(jnp.int32, (total_tok, total_tok), 1)
+
+    def as_column(row):
+        wide = jnp.where(pos_q == pos_k, row.astype(F32), 0.0)
+        return jnp.sum(wide, axis=-1, keepdims=True).astype(jnp.int32)
+
+    seg_row = seg_row_ref[...]
+    owner_row = jnp.zeros(seg_row.shape, jnp.int32)
+    for r in range(request_ref.shape[0]):
+        slot = jnp.int32(0)
+        for g in range(slot_ref.shape[0]):
+            slot = jnp.where(request_ref[r] == g, slot_ref[g], slot)
+        owner_row = jnp.where(seg_row == r, slot, owner_row)
+    mask = (as_column(seg_row) == seg_row) & (pos_k <= pos_q)
+    mine = as_column(owner_row) == s
     loads[1].wait()
     loads[2].wait()
-
-    all_q = qkv[:, :tok_seq].reshape(total_tok, cols)
-    all_k = qkv[:, tok_seq : 2 * tok_seq].reshape(total_tok, cols)
-    all_v = qkv[:, 2 * tok_seq :].reshape(total_tok, cols)
-    pos_q = lax.broadcasted_iota(jnp.int32, (total_tok, total_tok), 0)
-    pos_k = lax.broadcasted_iota(jnp.int32, (total_tok, total_tok), 1)
-    mask = (cols_ref[:, 0:1] == seg_row_ref[...]) & (pos_k <= pos_q)
-    mine = cols_ref[:, 1:2] == s
+    for copy in qv_copies + sums_copies + ks_copies:
+        copy.wait_recv()
+
+    all_q = qv[:, :tok_seq].reshape(total_tok, cols)
+    all_v = qv[:, tok_seq:].reshape(total_tok, cols)
+    all_k = ks[...].reshape(total_tok, cols)
+    scale_q = jnp.concatenate([inverse_columns(sums_grid[k])[:tok_seq] for k in range(S)], axis=0)
+    scale_q = scale_q * HD ** (-0.5)
     heads = []
     for h in range(cols // HD):
         part = slice(h * HD, (h + 1) * HD)
         q_h = all_q[:, part]
-        pre = lax.dot_general(q_h, pk[:, part], nt, preferred_element_type=F32) * HD ** (-0.5)
-        suf = lax.dot_general(q_h, all_k[:, part], nt, preferred_element_type=F32) * HD ** (-0.5)
+        pre = lax.dot_general(q_h, pk[:, part], nt, preferred_element_type=F32) * scale_q
+        suf = lax.dot_general(q_h, all_k[:, part], nt, preferred_element_type=F32) * scale_q
         suf = jnp.where(mask, suf, -1e30)
         top = jnp.maximum(
             jnp.max(pre, axis=-1, keepdims=True), jnp.max(suf, axis=-1, keepdims=True)
@@ -447,7 +472,7 @@
         attn_sum = attn_sum + rs_in[k].astype(F32)
     attn_sum = jnp.concatenate([attn_sum[:tok], attn_sum[tok:]], axis=-1)
     mixed = (tokens + attn_sum).astype(BF16).astype(F32)
-    expert_in = rms(mixed, mlp_gain_ref[...].astype(F32))
+    expert_in = rms(mixed, mlp_gain_ref[...].astype(F32).reshape(1, width))
 
     half = width // 2
     grid_a[c, x, y, z] = pack_rows(expert_in[None, :, :half])[0]
@@ -475,7 +500,7 @@
     expert = exp_local * t + s // (S // exp_local)
     blocks = 4 * NZ
 
-    def run_half(side):
+    def activity(side):
         block_a = grid_a[side].reshape(blocks, 2 * tok, half // 2)
         raw_b = grid_b[side]
         block_b = jnp.concatenate([raw_b[j, i] for i in range(2) for j in range(2)], axis=0)
@@ -483,24 +508,33 @@
         gated = jnp.dot(inputs, wg[...], preferred_element_type=F32)
         upward = jnp.dot(inputs, wu[...], preferred_element_type=F32)
         act = (gated / (1.0 + jnp.exp(-gated)) * upward).astype(BF16)
-        result = jnp.dot(act, wd[...], preferred_element_type=F32)
         table = gate_grid[side].reshape(blocks * tok, 128)
         lanes = lax.broadcasted_iota(jnp.int32, table.shape, 1)
-        scale = jnp.sum(jnp.where(lanes == expert, table, 0.0), axis=-1, keepdims=True)
-        result = (result * scale).reshape(blocks, tok, width)
-        res_a[side] = pack_rows(result[:, :, :half]).reshape(2, 2, NZ, 2 * tok, half // 2)
-        packed_b = pack_rows(result[:, :, half:])
+        return act, jnp.sum(jnp.where(lanes == expert, table, 0.0), axis=-1, keepdims=True)
+
+    def down_a(side, act, scale):
+        result = jnp.dot(act, wd[:, :half], preferred_element_type=F32) * scale
+        packed = pack_rows(result.reshape(blocks, tok, half))
+        res_a[side] = packed.reshape(2, 2, NZ, 2 * tok, half // 2)
+
+    def down_b(side, act, scale):
+        result = jnp.dot(act, wd[:, half:], preferred_element_type=F32) * scale
+        packed = pack_rows(result.reshape(blocks, tok, half))
         for i in range(2):
             for j in range(2):
                 first = (i * 2 + j) * NZ
-                res_b[side, j, i] = packed_b[first : first + NZ]
+                res_b[side, j, i] = packed[first : first + NZ]
 
     core_a.wait_recv()
     core_b.wait_recv()
-    run_half(1 - c)
+    act, scale = activity(1 - c)
+    down_a(1 - c, act, scale)
     rcore_a = send(res_a.at[1 - c], rc_a, ra_ss.at[0], ra_rs.at[0], peer_c)
+    down_b(1 - c, act, scale)
     rcore_b = send(res_b.at[1 - c], rc_b, rb_ss.at[0], rb_rs.at[0], peer_c)
-    run_half(c)
+    act, scale = activity(c)
+    down_a(c, act, scale)
+    down_b(c, act, scale)
 
     def added(first, second):
         return (first.astype(F32) + second.astype(F32)).astype(BF16)
@@ -554,15 +588,6 @@
     tok_seq = tok * T
     slots = prefix_keys.shape[1]
     units = w_gate.shape[2]
-    request = jnp.arange(request_group.shape[0], dtype=jnp.int32)
-    group = jnp.arange(prefix_owner.shape[0], dtype=jnp.int32)
-    owner_of_request = jnp.sum(
-        jnp.where(request_group[:, None] == group[None, :], prefix_owner[None, :], 0), axis=1
-    )
-    owner = jnp.sum(
-        jnp.where(segments[:, None] == request[None, :], owner_of_request[None, :], 0), axis=1
-    )
-    columns = jnp.stack([segments, owner], axis=1)
     vm, dma = pltpu.VMEM, pltpu.SemaphoreType.DMA
     quarter = width // 4
     blk = (2 * tok, quarter)
@@ -573,36 +598,49 @@
         vm((slots, cols), BF16), vm((slots, cols), BF16),
         vm((width, units), BF16), vm((width, units), BF16), vm((units, width), BF16),
         vm((T, 2 * tok, width // 2), BF16), vm((T, 8, 2 * tok_seq), F32),
-        vm((S, 3 * tok_seq, cols), BF16), vm((S, tok_seq, cols), BF16), vm((S, tok_seq, cols), BF16),
+        vm((S, 8, 2 * tok_seq), F32), vm((S, 2 * tok_seq, cols), BF16),
+        *[vm((S, tok_seq, cols), BF16)] * 3,
         vm((T, 2 * tok, width // 2), BF16), vm((T, 2 * tok, width // 2), BF16),
         grid, grid, vm((2, 2, 2, NZ, tok, 128), F32),
         grid, grid,
         *pair(2, 2, NZ), *pair(2, 2, NZ), *pair(2, NZ),
         *pair(2, NZ), *pair(NZ), *pair(NZ), *pair(NZ),
         dma((7,)),
-        *[dma((T,))] * 4, *[dma((S,))] * 4, *[dma((T,))] * 2,
+        *[dma((T,))] * 4, *[dma((S,))] * 8, *[dma((T,))] * 2,
         *[dma((8,))] * 10,
     ]
     in_vmem = pl.BlockSpec(memory_space=pltpu.VMEM)
+    in_smem = pl.BlockSpec(memory_space=pltpu.SMEM)
     in_any = pl.BlockSpec(memory_space=pl.ANY)
-    return pl.pallas_call(
+    results = pl.pallas_call(
         functools.partial(layer_kernel, (S, T, NZ, EXP_DEV)),
         out_shape=(
             jax.ShapeDtypeStruct((tok, width), BF16),
             jax.ShapeDtypeStruct((tok_seq, cols), BF16),
             jax.ShapeDtypeStruct((tok_seq, cols), BF16),
         ),
-        in_specs=[in_vmem] * 9 + [in_any] * 7,
+        in_specs=[in_vmem] * 6 + [in_smem] * 2 + [in_vmem] * 2 + [in_any] * 7,
         out_specs=(in_vmem,) * 3,
         scratch_shapes=scratch,
         compiler_params=pltpu.CompilerParams(
             collective_id=0, has_side_effects=True, vmem_limit_bytes=56 * 2**20
         ),
     )(
-        tokens, attn_gain[None], q_gain[None], k_gain[None], mlp_gain[None],
-        segments[None], columns, expert_ids, gate_weights,
+        tokens, attn_gain, q_gain, k_gain, mlp_gain,
+        segments[None], request_group, prefix_owner, expert_ids, gate_weights,
         jnp.transpose(w_qkv, (1, 0, 2)), w_out, prefix_keys, prefix_values, w_gate, w_up, w_down,
     )
+    return pl.pallas_call(
+        hand_on,
+        out_shape=tuple(jax.ShapeDtypeStruct(r.shape, r.dtype) for r in results),
+        in_specs=[in_vmem] * 3,
+        out_specs=(in_vmem,) * 3,
+    )(*results)
+
+
+def hand_on(*refs):
+    for source, target in zip(refs[:3], refs[3:]):
+        target[...] = source[...]
 
 
 def whole_heads(*arrays):

time: 81.7 us -> 70.3 us (0.86)
  local copies, waits for them, and re-layouts: 9.9 us -> 0 us
  other arithmetic: 2.21 us -> 0 us
  Pallas kernels: 68.5 us -> 69.4 us
    broadcast_in_dim x4 -> x0, local copies, waits for them, and re-layouts: 4.99 us -> none  [the longest x1 1.29 us: local_kernel(): attn_gain[None]]
    unnamed x3 -> x0, local copies, waits for them, and re-layouts: 4.12 us -> none
    reduce_sum x2 -> x0, other arithmetic: 1.52 us -> none  [the longest x1 0.76 us: local_kernel(): jnp.sum(jnp.where(segments[:, None] == request[None, :], owner_of_request...]
    pallas_call x0 -> x1, Pallas kernels: none -> 1.43 us  [local_kernel(): pl.pallas_call(hand_on, out_shape=tuple((jax.ShapeDtypeStruct(r.shape, r....]
where the time goes in v2:
time: 70.3 us; the launch traced here: 70 us
  Pallas kernels  69.4 us (99%)
    pallas_call x1, Pallas kernels, local_kernel(): pl.pallas_call(functools.partial(layer_kernel, (S, T, NZ, EXP_DEV)), out_...  68 us
    pallas_call x1, Pallas kernels, local_kernel(): pl.pallas_call(hand_on, out_shape=tuple((jax.ShapeDtypeStruct(r.shape, r....  1.43 us

profile of v2, /device:TPU:0, one launch (start us, length us, event | category | flops | bytes accessed | tf_op | source)
XLA Modules:
  0.0 70.0 jit_solution(1385803858573901764)
XLA Ops:
  0.6 68.0 %shard_map.184 = (bf16[8,2048]{1,0:T(8,128)(2,1)}, bf16[64,256]{1,0:T(8,128)(2,1)}, bf16[64,256]{1,0:T(8,128)(2,1)}) custom-call(bf16[8,2048]{1,0:T(8,128)(2,1)} %tokens_ref.1, bf16[2048]{0:T(1024)(128)(2,1)} %attn_gain_ref.1, bf16[256]{0:T(256)(128)(2,1)} %q_gain_ref.1, bf16[256]{0:T(256)(128)(2,1)} %k_gain_ref.1, bf16[2048]{0:T(1024)(128)(2,1)} %mlp_gain_ref.1, ...), custom_call_target="tpu_custom_call" | custom-call | tf_op jit(solution)/shard_map/pallas_call | solution.py:615
  68.6 1.4 %shard_map.185 = (bf16[8,2048]{1,0:T(8,128)(2,1)}, bf16[64,256]{1,0:T(8,128)(2,1)}, bf16[64,256]{1,0:T(8,128)(2,1)}) custom-call(bf16[8,2048]{1,0:T(8,128)(2,1)} %get-tuple-element.6.refs_0_, bf16[64,256]{1,0:T(8,128)(2,1)} %get-tuple-element.7.refs_1_, bf16[64,256]{1,0:T(8,128)(2,1)} %get-tuple-element.8.refs_2_), custom_call_target="tpu_custom_call" | custom-call | tf_op jit(solution)/shard_map/pallas_call | solution.py:633

commit v3 on v2

--- a/solution.py
+++ b/solution.py
@@ -326,8 +326,11 @@
     def to_tensor(k):
         return (s, (t + k) % T)
 
-    def to_seq(k):
-        return ((s + k) % S, t)
+    def seq_peer(d):
+        return ((x + d // 2) % 2) * 2 + (c + d % 2) % 2
+
+    def to_seq(d):
+        return (seq_peer(d), t)
 
     peer_x = ((1 - x) * 2 + c, t)
     peer_c = (x * 2 + 1 - c, t)
@@ -406,13 +409,6 @@
     ks_copies = [send(ks.at[s], ks.at[s], ks_ss.at[k], ks_rs.at[k], to_seq(k)) for k in range(1, S)]
     gg_y.wait_recv()
     gg_x = send(gate_grid.at[c, x], gate_grid.at[c, x], gg_ss.at[5], gg_rs.at[5], peer_x)
-    pos_q = lax.broadcasted_iota(jnp.int32, (total_tok, total_tok), 0)
-    pos_k = lax.broadcasted_iota(jnp.int32, (total_tok, total_tok), 1)
-
-    def as_column(row):
-        wide = jnp.where(pos_q == pos_k, row.astype(F32), 0.0)
-        return jnp.sum(wide, axis=-1, keepdims=True).astype(jnp.int32)
-
     seg_row = seg_row_ref[...]
     owner_row = jnp.zeros(seg_row.shape, jnp.int32)
     for r in range(request_ref.shape[0]):
@@ -420,39 +416,80 @@
         for g in range(slot_ref.shape[0]):
             slot = jnp.where(request_ref[r] == g, slot_ref[g], slot)
         owner_row = jnp.where(seg_row == r, slot, owner_row)
-    mask = (as_column(seg_row) == seg_row) & (pos_k <= pos_q)
-    mine = as_column(owner_row) == s
+    chip_tok = 2 * tok_seq
+    own_chip, next_chip = x, 1 - x
+
+    def masks(chip):
+        pos_q = lax.broadcasted_iota(jnp.int32, (chip_tok, total_tok), 0) + chip * chip_tok
+        pos_k = lax.broadcasted_iota(jnp.int32, (chip_tok, total_tok), 1)
+
+        def as_column(row):
+            wide = jnp.where(pos_q == pos_k, row.astype(F32), 0.0)
+            return jnp.sum(wide, axis=-1, keepdims=True).astype(jnp.int32)
+
+        mask = (as_column(seg_row) == seg_row) & (pos_k <= pos_q)
+        return mask, as_column(owner_row) == s
+
+    def queries_of(chip):
+        rows = qv[pl.ds(2 * chip, 2), :tok_seq].reshape(chip_tok, cols)
+        sums = sums_grid[pl.ds(2 * chip, 2)]
+        scale = jnp.concatenate([inverse_columns(sums[k])[:tok_seq] for k in range(2)], axis=0)
+        return rows, scale * HD ** (-0.5)
+
+    def prefix_part(rows, scale):
+        parts = []
+        for h in range(cols // HD):
+            part = slice(h * HD, (h + 1) * HD)
+            pre = lax.dot_general(rows[:, part], pk[:, part], nt, preferred_element_type=F32)
+            pre = pre * scale
+            top = jnp.max(pre, axis=-1, keepdims=True)
+            pre = jnp.exp(pre - top)
+            total = jnp.sum(pre, axis=-1, keepdims=True)
+            mix = jnp.dot(pre.astype(BF16), pv[:, part], preferred_element_type=F32)
+            parts.append((top, total, mix))
+        return parts
+
+    def with_suffix(chip, rows, scale, parts, mask, mine):
+        all_v = qv[:, tok_seq:].reshape(total_tok, cols)
+        all_k = ks[...].reshape(total_tok, cols)
+        heads = []
+        for h in range(cols // HD):
+            part = slice(h * HD, (h + 1) * HD)
+            top_p, total_p, mix_p = parts[h]
+            suf = lax.dot_general(rows[:, part], all_k[:, part], nt, preferred_element_type=F32)
+            suf = jnp.where(mask, suf * scale, -1e30)
+            top = jnp.maximum(top_p, jnp.max(suf, axis=-1, keepdims=True))
+            suf = jnp.where(mask, jnp.exp(suf - top), 0.0)
+            factor = jnp.exp(top_p - top)
+            total = total_p * factor + jnp.sum(suf, axis=-1, keepdims=True)
+            mix = jnp.dot(suf.astype(BF16), all_v[:, part], preferred_element_type=F32)
+            mix = mix_p * factor + mix
+            heads.append(jnp.where(mine, mix / total, 0.0).astype(BF16))
+        out = jnp.concatenate(heads, axis=-1).reshape(2, tok_seq, cols)
+        att_snd[pl.ds(2 * chip, 2)] = out
+
+    mask_own, mine_own = masks(own_chip)
+    mask_next, mine_next = masks(next_chip)
     loads[1].wait()
     loads[2].wait()
-    for copy in qv_copies + sums_copies + ks_copies:
-        copy.wait_recv()
-
-    all_q = qv[:, :tok_seq].reshape(total_tok, cols)
-    all_v = qv[:, tok_seq:].reshape(total_tok, cols)
-    all_k = ks[...].reshape(total_tok, cols)
-    scale_q = jnp.concatenate([inverse_columns(sums_grid[k])[:tok_seq] for k in range(S)], axis=0)
-    scale_q = scale_q * HD ** (-0.5)
-    heads = []
-    for h in range(cols // HD):
-        part = slice(h * HD, (h + 1) * HD)
-        q_h = all_q[:, part]
-        pre = lax.dot_general(q_h, pk[:, part], nt, preferred_element_type=F32) * scale_q
-        suf = lax.dot_general(q_h, all_k[:, part], nt, preferred_element_type=F32) * scale_q
-        suf = jnp.where(mask, suf, -1e30)
-        top = jnp.maximum(
-            jnp.max(pre, axis=-1, keepdims=True), jnp.max(suf, axis=-1, keepdims=True)
-        )
-        pre = jnp.exp(pre - top)
-        suf = jnp.where(mask, jnp.exp(suf - top), 0.0)
-        total = jnp.sum(pre, axis=-1, keepdims=True) + jnp.sum(suf, axis=-1, keepdims=True)
-        mix = jnp.dot(pre.astype(BF16), pv[:, part], preferred_element_type=F32)
-        mix = mix + jnp.dot(suf.astype(BF16), all_v[:, part], preferred_element_type=F32)
-        heads.append(jnp.where(mine, mix / total, 0.0).astype(BF16))
-    att_snd[...] = jnp.concatenate(heads, axis=-1).reshape(S, tok_seq, cols)
-    att_copies = [
-        send(att_snd.at[(s + k) % S], att_in.at[k], att_ss.at[k], att_rs.at[k], to_seq(k))
-        for k in range(1, S)
-    ]
+    qv_copies[0].wait_recv()
+    sums_copies[0].wait_recv()
+    rows_own, scale_own = queries_of(own_chip)
+    parts_own = prefix_part(rows_own, scale_own)
+    for copy in qv_copies[1:] + sums_copies[1:]:
+        copy.wait_recv()
+    rows_next, scale_next = queries_of(next_chip)
+    parts_next = prefix_part(rows_next, scale_next)
+    for copy in ks_copies:
+        copy.wait_recv()
+
+    def send_attended(d):
+        return send(att_snd.at[seq_peer(d)], att_in.at[d], att_ss.at[d], att_rs.at[d], to_seq(d))
+
+    with_suffix(next_chip, rows_next, scale_next, parts_next, mask_next, mine_next)
+    far_copies = [send_attended(2), send_attended(3)]
+    with_suffix(own_chip, rows_own, scale_own, parts_own, mask_own, mine_own)
+    att_copies = [send_attended(1)] + far_copies
     gg_x.wait_recv()
     gg_c = send(gate_grid.at[c], gate_grid.at[c], gg_ss.at[6], gg_rs.at[6], peer_c)
     attended = att_snd[s].astype(F32)
@@ -478,22 +515,44 @@
     grid_a[c, x, y, z] = pack_rows(expert_in[None, :, :half])[0]
     grid_b[c, y, x, z] = pack_rows(expert_in[None, :, half:])[0]
     mine_a, mine_b = grid_a.at[c, x, y, z], grid_b.at[c, y, x, z]
-    z_a = [send(mine_a, mine_a, ga_ss.at[k], ga_rs.at[k], to_z(k)) for k in range(1, NZ)]
-    z_b = [send(mine_b, mine_b, gb_ss.at[k], gb_rs.at[k], to_z(k)) for k in range(1, NZ)]
-    for copy in z_a:
-        copy.wait_recv()
-    two_a = send(grid_a.at[c, x, y], grid_a.at[c, x, y], ga_ss.at[4], ga_rs.at[4], peer_y)
-    for copy in z_b:
-        copy.wait_recv()
-    two_b = send(grid_b.at[c, y, x], grid_b.at[c, y, x], gb_ss.at[4], gb_rs.at[4], peer_x)
-    two_a.wait_recv()
-    one_a = send(grid_a.at[c, x], grid_a.at[c, x], ga_ss.at[5], ga_rs.at[5], peer_x)
-    two_b.wait_recv()
-    one_b = send(grid_b.at[c, y], grid_b.at[c, y], gb_ss.at[5], gb_rs.at[5], peer_y)
-    one_a.wait_recv()
-    core_a = send(grid_a.at[c], grid_a.at[c], ga_ss.at[6], ga_rs.at[6], peer_c)
-    one_b.wait_recv()
-    core_b = send(grid_b.at[c], grid_b.at[c], gb_ss.at[6], gb_rs.at[6], peer_c)
+
+    def z_stage(own, ss, rs):
+        return [send(own, own, ss.at[k], rs.at[k], to_z(k)) for k in range(1, NZ)]
+
+    def hand_block(grid, i, j, k, ss, rs, to):
+        block = grid.at[c, i, j, (z - k + NZ) % NZ]
+        return send(block, block, ss.at[4 + k], rs.at[4 + k], to)
+
+    z_a = z_stage(mine_a, ga_ss, ga_rs)
+    z_b = z_stage(mine_b, gb_ss, gb_rs)
+    two_a = [hand_block(grid_a, x, y, 0, ga_ss, ga_rs, peer_y)]
+    two_b = [hand_block(grid_b, y, x, 0, gb_ss, gb_rs, peer_x)]
+    for k in (1, NZ - 1, *range(2, NZ - 1)):
+        z_a[k - 1].wait_recv()
+        two_a.append(hand_block(grid_a, x, y, k, ga_ss, ga_rs, peer_y))
+        z_b[k - 1].wait_recv()
+        two_b.append(hand_block(grid_b, y, x, k, gb_ss, gb_rs, peer_x))
+
+    def hand_row(grid, i, j, n, ss, rs, to):
+        row = grid.at[c, i, j]
+        return send(row, row, ss.at[n], rs.at[n], to)
+
+    one_a = [hand_row(grid_a, x, y, 8, ga_ss, ga_rs, peer_x)]
+    one_b = [hand_row(grid_b, y, x, 8, gb_ss, gb_rs, peer_y)]
+    for copy in two_a:
+        copy.wait_recv()
+    one_a.append(hand_row(grid_a, x, 1 - y, 9, ga_ss, ga_rs, peer_x))
+    core_a = [send(grid_a.at[c, x], grid_a.at[c, x], ga_ss.at[10], ga_rs.at[10], peer_c)]
+    for copy in two_b:
+        copy.wait_recv()
+    one_b.append(hand_row(grid_b, y, 1 - x, 9, gb_ss, gb_rs, peer_y))
+    core_b = [send(grid_b.at[c, y], grid_b.at[c, y], gb_ss.at[10], gb_rs.at[10], peer_c)]
+    for copy in one_a:
+        copy.wait_recv()
+    core_a.append(send(grid_a.at[c, 1 - x], grid_a.at[c, 1 - x], ga_ss.at[11], ga_rs.at[11], peer_c))
+    for copy in one_b:
+        copy.wait_recv()
+    core_b.append(send(grid_b.at[c, 1 - y], grid_b.at[c, 1 - y], gb_ss.at[11], gb_rs.at[11], peer_c))
     for load in loads[4:]:
         load.wait()
     gg_c.wait_recv()
@@ -525,8 +584,8 @@
                 first = (i * 2 + j) * NZ
                 res_b[side, j, i] = packed[first : first + NZ]
 
-    core_a.wait_recv()
-    core_b.wait_recv()
+    for copy in core_a + core_b:
+        copy.wait_recv()
     act, scale = activity(1 - c)
     down_a(1 - c, act, scale)
     rcore_a = send(res_a.at[1 - c], rc_a, ra_ss.at[0], ra_rs.at[0], peer_c)
@@ -541,28 +600,36 @@
 
     rcore_a.wait_recv()
     s1_a[...] = added(res_a[c], rc_a[...])
-    rone_a = send(s1_a.at[1 - x], r1_a, ra_ss.at[1], ra_rs.at[1], peer_x)
+
+    def row_out(s1, r1, i, j, n, ss, rs, to):
+        return send(s1.at[1 - i, j], r1.at[j], ss.at[n], rs.at[n], to)
+
+    rone_a = [row_out(s1_a, r1_a, x, 1 - y, 1, ra_ss, ra_rs, peer_x)]
+    rone_a.append(row_out(s1_a, r1_a, x, y, 2, ra_ss, ra_rs, peer_x))
     rcore_b.wait_recv()
     s1_b[...] = added(res_b[c], rc_b[...])
-    rone_b = send(s1_b.at[1 - y], r1_b, rb_ss.at[1], rb_rs.at[1], peer_y)
-    rone_b.wait_recv()
-    s2_b[...] = added(s1_b[y], r1_b[...])
-    rone_a.wait_recv()
-    s2_a[...] = added(s1_a[x], r1_a[...])
-    rtwo_a = send(s2_a.at[1 - y], r2_a, ra_ss.at[2], ra_rs.at[2], peer_y)
-    rtwo_b = send(s2_b.at[1 - x], r2_b, rb_ss.at[2], rb_rs.at[2], peer_x)
+    rone_b = [row_out(s1_b, r1_b, y, 1 - x, 1, rb_ss, rb_rs, peer_y)]
+    rone_b.append(row_out(s1_b, r1_b, y, x, 2, rb_ss, rb_rs, peer_y))
+    rone_a[0].wait_recv()
+    s2_a[1 - y] = added(s1_a[x, 1 - y], r1_a[1 - y])
+    rtwo_a = send(s2_a.at[1 - y], r2_a, ra_ss.at[3], ra_rs.at[3], peer_y)
+    rone_b[0].wait_recv()
+    s2_b[1 - x] = added(s1_b[y, 1 - x], r1_b[1 - x])
+    rtwo_b = send(s2_b.at[1 - x], r2_b, rb_ss.at[3], rb_rs.at[3], peer_x)
+    rone_a[1].wait_recv()
+    s2_a[y] = added(s1_a[x, y], r1_a[y])
+    rone_b[1].wait_recv()
+    s2_b[x] = added(s1_b[y, x], r1_b[x])
+
+    def z_out(s3, r3, k, ss, rs):
+        return send(s3.at[(z + k) % NZ], r3.at[k], ss.at[3 + k], rs.at[3 + k], to_z(k))
+
     rtwo_a.wait_recv()
     s3_a[...] = added(s2_a[y], r2_a[...])
-    rz_a = [
-        send(s3_a.at[(z + k) % NZ], r3_a.at[k], ra_ss.at[2 + k], ra_rs.at[2 + k], to_z(k))
-        for k in range(1, NZ)
-    ]
+    rz_a = [z_out(s3_a, r3_a, k, ra_ss, ra_rs) for k in range(1, NZ)]
     rtwo_b.wait_recv()
     s3_b[...] = added(s2_b[x], r2_b[...])
-    rz_b = [
-        send(s3_b.at[(z + k) % NZ], r3_b.at[k], rb_ss.at[2 + k], rb_rs.at[2 + k], to_z(k))
-        for k in range(1, NZ)
-    ]
+    rz_b = [z_out(s3_b, r3_b, k, rb_ss, rb_rs) for k in range(1, NZ)]
     sum_a = s3_a[z].astype(F32)
     sum_b = s3_b[z].astype(F32)
     for k in range(1, NZ):
@@ -607,7 +674,7 @@
         *pair(2, NZ), *pair(NZ), *pair(NZ), *pair(NZ),
         dma((7,)),
         *[dma((T,))] * 4, *[dma((S,))] * 8, *[dma((T,))] * 2,
-        *[dma((8,))] * 10,
+        *[dma((8,))] * 2, *[dma((NZ + 8,))] * 8,
     ]
     in_vmem = pl.BlockSpec(memory_space=pltpu.VMEM)
     in_smem = pl.BlockSpec(memory_space=pltpu.SMEM)

time: 70.3 us -> 65.6 us (0.933)
  Pallas kernels: 69.4 us -> 64.7 us
    pallas_call x1, Pallas kernels: 68 us -> 63.3 us  [local_kernel(): pl.pallas_call(functools.partial(layer_kernel, (S, T, NZ, EXP_DEV)), out_...]
where the time goes in v3:
time: 65.6 us; the launch traced here: 65.4 us
  Pallas kernels  64.7 us (99%)
    pallas_call x1, Pallas kernels, local_kernel(): pl.pallas_call(functools.partial(layer_kernel, (S, T, NZ, EXP_DEV)), out_...  63.3 us
    pallas_call x1, Pallas kernels, local_kernel(): pl.pallas_call(hand_on, out_shape=tuple((jax.ShapeDtypeStruct(r.shape, r....  1.43 us

profile of v3, /device:TPU:0, one launch (start us, length us, event | category | flops | bytes accessed | tf_op | source)
XLA Modules:
  0.0 65.4 jit_solution(7197094543990297404)
XLA Ops:
  0.6 63.3 %shard_map.184 = (bf16[8,2048]{1,0:T(8,128)(2,1)}, bf16[64,256]{1,0:T(8,128)(2,1)}, bf16[64,256]{1,0:T(8,128)(2,1)}) custom-call(bf16[8,2048]{1,0:T(8,128)(2,1)} %tokens_ref.1, bf16[2048]{0:T(1024)(128)(2,1)} %attn_gain_ref.1, bf16[256]{0:T(256)(128)(2,1)} %q_gain_ref.1, bf16[256]{0:T(256)(128)(2,1)} %k_gain_ref.1, bf16[2048]{0:T(1024)(128)(2,1)} %mlp_gain_ref.1, ...), custom_call_target="tpu_custom_call" | custom-call | tf_op jit(solution)/shard_map/pallas_call | solution.py:682
  64.0 1.4 %shard_map.185 = (bf16[8,2048]{1,0:T(8,128)(2,1)}, bf16[64,256]{1,0:T(8,128)(2,1)}, bf16[64,256]{1,0:T(8,128)(2,1)}) custom-call(bf16[8,2048]{1,0:T(8,128)(2,1)} %get-tuple-element.6.refs_0_, bf16[64,256]{1,0:T(8,128)(2,1)} %get-tuple-element.7.refs_1_, bf16[64,256]{1,0:T(8,128)(2,1)} %get-tuple-element.8.refs_2_), custom_call_target="tpu_custom_call" | custom-call | tf_op jit(solution)/shard_map/pallas_call | solution.py:700

commit v4 on v3

--- a/solution.py
+++ b/solution.py
@@ -352,14 +352,24 @@
         dense = dense + jnp.where(ids_ref[:, k : k + 1] == lane, gates_ref[:, k : k + 1], 0.0)
     gate_grid[c, x, y, z] = dense
     pl.semaphore_wait(barrier, T + S - 2)
-    ag_copies = [
-        send(ag.at[t], ag.at[t], ag_ss.at[k], ag_rs.at[k], to_tensor(k)) for k in range(1, T)
-    ]
+    far_first = (NZ // 2, 1, *range(NZ // 2 + 1, NZ), *range(2, NZ // 2))
+    ag_z = {
+        k: send(ag.at[t], ag.at[t], ag_ss.at[k], ag_rs.at[k], to_z(k)) for k in far_first
+    }
+
+    def ag_hand(k):
+        block = ag.at[((z - k + NZ) % NZ) * 2 + y]
+        return send(block, block, ag_ss.at[NZ + k], ag_rs.at[NZ + k], peer_y)
+
+    ag_y = [ag_hand(0)]
     gg_z = [
         send(gate_grid.at[c, x, y, z], gate_grid.at[c, x, y, z], gg_ss.at[k], gg_rs.at[k], to_z(k))
         for k in range(1, NZ)
     ]
-    for copy in ag_copies:
+    for k in (1, NZ - 1, *range(2, NZ - 1)):
+        ag_z[k].wait_recv()
+        ag_y.append(ag_hand(k))
+    for copy in ag_y:
         copy.wait_recv()
     rows = unpack_rows(ag[...]).astype(BF16)
     loads[0].wait()
@@ -499,14 +509,30 @@
     loads[3].wait()
     partial = jnp.dot(attended.astype(BF16), wout[...], preferred_element_type=F32)
     rs_snd[...] = pack_rows(partial.reshape(T, tok, width))
-    rs_copies = [
-        send(rs_snd.at[(t + k) % T], rs_in.at[k], rs_ss.at[k], rs_rs.at[k], to_tensor(k))
-        for k in range(1, T)
-    ]
-    attn_sum = rs_snd[t].astype(F32)
-    for k in range(1, T):
-        rs_copies[k - 1].wait_recv()
-        attn_sum = attn_sum + rs_in[k].astype(F32)
+    def over_y(k):
+        z_to = (z + k) % NZ
+        return send(
+            rs_snd.at[z_to * 2 + 1 - y], rs_in.at[z_to], rs_ss.at[k], rs_rs.at[k], peer_y
+        )
+
+    def over_z(k):
+        mid = ((z + k) % NZ) * 2 + y
+        return send(rs_snd.at[mid], rs_in.at[NZ + k], rs_ss.at[NZ + k], rs_rs.at[NZ + k], to_z(k))
+
+    rs_y = {k: over_y(k) for k in (*far_first, 0)}
+    rs_z = []
+    for k in far_first:
+        rs_y[k].wait_recv()
+        z_to = (z + k) % NZ
+        mid = rs_snd[z_to * 2 + y].astype(F32) + rs_in[z_to].astype(F32)
+        rs_snd[z_to * 2 + y] = mid.astype(BF16)
+        rs_z.append(over_z(k))
+    rs_y[0].wait_recv()
+    attn_sum = rs_snd[t].astype(F32) + rs_in[z].astype(F32)
+    for copy in rs_z:
+        copy.wait_recv()
+    for k in range(1, NZ):
+        attn_sum = attn_sum + rs_in[NZ + k].astype(F32)
     attn_sum = jnp.concatenate([attn_sum[:tok], attn_sum[tok:]], axis=-1)
     mixed = (tokens + attn_sum).astype(BF16).astype(F32)
     expert_in = rms(mixed, mlp_gain_ref[...].astype(F32).reshape(1, width))
@@ -584,6 +610,7 @@
                 first = (i * 2 + j) * NZ
                 res_b[side, j, i] = packed[first : first + NZ]
 
+    act_own, scale_own = activity(c)
     for copy in core_a + core_b:
         copy.wait_recv()
     act, scale = activity(1 - c)
@@ -591,9 +618,8 @@
     rcore_a = send(res_a.at[1 - c], rc_a, ra_ss.at[0], ra_rs.at[0], peer_c)
     down_b(1 - c, act, scale)
     rcore_b = send(res_b.at[1 - c], rc_b, rb_ss.at[0], rb_rs.at[0], peer_c)
-    act, scale = activity(c)
-    down_a(c, act, scale)
-    down_b(c, act, scale)
+    down_a(c, act_own, scale_own)
+    down_b(c, act_own, scale_own)
 
     def added(first, second):
         return (first.astype(F32) + second.astype(F32)).astype(BF16)

time: 65.6 us -> 65.7 us (level)
  no operation moved by 1% of the time
where the time goes in v4:
time: 65.7 us; the launch traced here: 65.4 us
  Pallas kernels  64.8 us (99%)
    pallas_call x1, Pallas kernels, local_kernel(): pl.pallas_call(functools.partial(layer_kernel, (S, T, NZ, EXP_DEV)), out_...  63.3 us
    pallas_call x1, Pallas kernels, local_kernel(): pl.pallas_call(hand_on, out_shape=tuple((jax.ShapeDtypeStruct(r.shape, r....  1.43 us

profile of v4, /device:TPU:0, one launch (start us, length us, event | category | flops | bytes accessed | tf_op | source)
XLA Modules:
  0.0 65.4 jit_solution(756866234776688543)
XLA Ops:
  0.6 63.3 %shard_map.184 = (bf16[8,2048]{1,0:T(8,128)(2,1)}, bf16[64,256]{1,0:T(8,128)(2,1)}, bf16[64,256]{1,0:T(8,128)(2,1)}) custom-call(bf16[8,2048]{1,0:T(8,128)(2,1)} %tokens_ref.1, bf16[2048]{0:T(1024)(128)(2,1)} %attn_gain_ref.1, bf16[256]{0:T(256)(128)(2,1)} %q_gain_ref.1, bf16[256]{0:T(256)(128)(2,1)} %k_gain_ref.1, bf16[2048]{0:T(1024)(128)(2,1)} %mlp_gain_ref.1, ...), custom_call_target="tpu_custom_call" | custom-call | tf_op jit(solution)/shard_map/pallas_call | solution.py:708
  64.0 1.4 %shard_map.185 = (bf16[8,2048]{1,0:T(8,128)(2,1)}, bf16[64,256]{1,0:T(8,128)(2,1)}, bf16[64,256]{1,0:T(8,128)(2,1)}) custom-call(bf16[8,2048]{1,0:T(8,128)(2,1)} %get-tuple-element.6.refs_0_, bf16[64,256]{1,0:T(8,128)(2,1)} %get-tuple-element.7.refs_1_, bf16[64,256]{1,0:T(8,128)(2,1)} %get-tuple-element.8.refs_2_), custom_call_target="tpu_custom_call" | custom-call | tf_op jit(solution)/shard_map/pallas_call | solution.py:726

commit v5 on v3

--- a/solution.py
+++ b/solution.py
@@ -352,8 +352,9 @@
         dense = dense + jnp.where(ids_ref[:, k : k + 1] == lane, gates_ref[:, k : k + 1], 0.0)
     gate_grid[c, x, y, z] = dense
     pl.semaphore_wait(barrier, T + S - 2)
+    far_first = sorted(range(1, T), key=lambda k: abs(k - T // 2))
     ag_copies = [
-        send(ag.at[t], ag.at[t], ag_ss.at[k], ag_rs.at[k], to_tensor(k)) for k in range(1, T)
+        send(ag.at[t], ag.at[t], ag_ss.at[k], ag_rs.at[k], to_tensor(k)) for k in far_first
     ]
     gg_z = [
         send(gate_grid.at[c, x, y, z], gate_grid.at[c, x, y, z], gg_ss.at[k], gg_rs.at[k], to_z(k))
@@ -501,11 +502,12 @@
     rs_snd[...] = pack_rows(partial.reshape(T, tok, width))
     rs_copies = [
         send(rs_snd.at[(t + k) % T], rs_in.at[k], rs_ss.at[k], rs_rs.at[k], to_tensor(k))
-        for k in range(1, T)
+        for k in far_first
     ]
     attn_sum = rs_snd[t].astype(F32)
+    for copy in rs_copies:
+        copy.wait_recv()
     for k in range(1, T):
-        rs_copies[k - 1].wait_recv()
         attn_sum = attn_sum + rs_in[k].astype(F32)
     attn_sum = jnp.concatenate([attn_sum[:tok], attn_sum[tok:]], axis=-1)
     mixed = (tokens + attn_sum).astype(BF16).astype(F32)
@@ -584,6 +586,7 @@
                 first = (i * 2 + j) * NZ
                 res_b[side, j, i] = packed[first : first + NZ]
 
+    act_own, scale_own = activity(c)
     for copy in core_a + core_b:
         copy.wait_recv()
     act, scale = activity(1 - c)
@@ -591,9 +594,8 @@
     rcore_a = send(res_a.at[1 - c], rc_a, ra_ss.at[0], ra_rs.at[0], peer_c)
     down_b(1 - c, act, scale)
     rcore_b = send(res_b.at[1 - c], rc_b, rb_ss.at[0], rb_rs.at[0], peer_c)
-    act, scale = activity(c)
-    down_a(c, act, scale)
-    down_b(c, act, scale)
+    down_a(c, act_own, scale_own)
+    down_b(c, act_own, scale_own)
 
     def added(first, second):
         return (first.astype(F32) + second.astype(F32)).astype(BF16)

time: 65.6 us -> 64.8 us (0.988)
  Pallas kernels: 64.7 us -> 63.9 us
    pallas_call x1, Pallas kernels: 63.3 us -> 62.5 us  [local_kernel(): pl.pallas_call(functools.partial(layer_kernel, (S, T, NZ, EXP_DEV)), out_...]
where the time goes in v5:
time: 64.8 us; the launch traced here: 64.5 us
  Pallas kernels  63.9 us (99%)
  between operations  0.65 us (1%)
    pallas_call x1, Pallas kernels, local_kernel(): pl.pallas_call(functools.partial(layer_kernel, (S, T, NZ, EXP_DEV)), out_...  62.5 us
    pallas_call x1, Pallas kernels, local_kernel(): pl.pallas_call(hand_on, out_shape=tuple((jax.ShapeDtypeStruct(r.shape, r....  1.43 us

profile of v5, /device:TPU:0, one launch (start us, length us, event | category | flops | bytes accessed | tf_op | source)
XLA Modules:
  0.0 64.5 jit_solution(3301156342453310826)
XLA Ops:
  0.6 62.5 %shard_map.184 = (bf16[8,2048]{1,0:T(8,128)(2,1)}, bf16[64,256]{1,0:T(8,128)(2,1)}, bf16[64,256]{1,0:T(8,128)(2,1)}) custom-call(bf16[8,2048]{1,0:T(8,128)(2,1)} %tokens_ref.1, bf16[2048]{0:T(1024)(128)(2,1)} %attn_gain_ref.1, bf16[256]{0:T(256)(128)(2,1)} %q_gain_ref.1, bf16[256]{0:T(256)(128)(2,1)} %k_gain_ref.1, bf16[2048]{0:T(1024)(128)(2,1)} %mlp_gain_ref.1, ...), custom_call_target="tpu_custom_call" | custom-call | tf_op jit(solution)/shard_map/pallas_call | solution.py:684
  63.1 1.4 %shard_map.185 = (bf16[8,2048]{1,0:T(8,128)(2,1)}, bf16[64,256]{1,0:T(8,128)(2,1)}, bf16[64,256]{1,0:T(8,128)(2,1)}) custom-call(bf16[8,2048]{1,0:T(8,128)(2,1)} %get-tuple-element.6.refs_0_, bf16[64,256]{1,0:T(8,128)(2,1)} %get-tuple-element.7.refs_1_, bf16[64,256]{1,0:T(8,128)(2,1)} %get-tuple-element.8.refs_2_), custom_call_target="tpu_custom_call" | custom-call | tf_op jit(solution)/shard_map/pallas_call | solution.py:702
